TPU v7x, 256 devices: a whole 4x4x8 slice. The times are simulated.
256 devices in a mesh: ctx: 32 (over x, z), tp: 8 (over y, core).
Axes of the slice: x: 4, y: 4, z: 8, core: 2. Of those that a mesh axis runs over, the one named last changes fastest.
Arguments:
- query: bfloat16 [16384, 8192], P('ctx', 'tp'), may hold values from -2 to 2
- key_in: bfloat16 [16384, 8192], P('ctx', 'tp'), may hold values from -2 to 2
- value: bfloat16 [16384, 8192], P('ctx', 'tp'), may hold values from -6 to 6
- gate: bfloat16 [16384, 8192], P('ctx', 'tp'), may hold values from -6 to 6
- gain: float32 [8192], P('tp'), may hold values from 0.25 to 1.75
- grad_out: bfloat16 [16384, 8192], P('ctx', 'tp'), may hold values from -6 to 6
Outputs:
- gated: bfloat16 [16384, 8192], P('ctx', 'tp')
- grad_query: bfloat16 [16384, 8192], P('ctx', 'tp')
- grad_key: bfloat16 [16384, 8192], P('ctx', 'tp')
- grad_value: bfloat16 [16384, 8192], P('ctx', 'tp')
- grad_gate: bfloat16 [16384, 8192], P('ctx', 'tp')
- gain_gradient: float32 [8192], P('tp')
All inputs are finite; a program needn't handle non-finite values.
Results may differ from a plain program's by a relative error of at most 0.0058.
Values sent between devices are 32-bit elements; how exact they have to be, the bound alone decides.
A program may use at most 128 MiB of HBM per device.

v0:
```python
import jax
import jax.numpy as jnp
from jax import lax
from jax.sharding import PartitionSpec as P

ATTENTION_HEADS = 64
HEAD_WIDTH = 128


def prefix_2(shard, axis, combine, identity, reverse):
    size, place = (lax.axis_size(axis), lax.axis_index(axis))
    everything = lax.all_gather(shard, axis)
    start = jnp.broadcast_to(jnp.asarray(identity, shard.dtype), shard.shape)

    def hop(k, before):
        at = size - 1 - k if reverse else k
        reached = at > place if reverse else at < place
        new = combine(before, everything[at])
        return jnp.where(reached, new, before)

    return lax.fori_loop(0, size, hop, start)


def add_states(earlier, later):
    return earlier + later


def body(query, key_in, value, gate, gain, grad_out):
    tok_rows = query.shape[0]
    heads_dev = query.shape[1] // HEAD_WIDTH
    q_heads = query.reshape(tok_rows, heads_dev, HEAD_WIDTH)
    k_heads = key_in.reshape(tok_rows, heads_dev, HEAD_WIDTH)
    v_heads = value.reshape(tok_rows, heads_dev, HEAD_WIDTH)
    local = jnp.einsum("thd,the->hde", k_heads, v_heads, preferred_element_type=jnp.float32)
    zero_state = jnp.zeros_like(local)
    prefix = prefix_2(local, "ctx", add_states, zero_state, False)
    prefix_b = prefix.astype(jnp.bfloat16)
    positions = jnp.arange(tok_rows)
    causal = (positions[:, None] >= positions[None, :])[None]
    scores = jnp.einsum("thd,shd->hts", q_heads, k_heads, preferred_element_type=jnp.float32)
    probs = jnp.where(causal, scores, 0.0).astype(jnp.bfloat16)
    attention_output = jnp.einsum(
        "hts,she->the", probs, v_heads, preferred_element_type=jnp.float32
    )
    attention_output = attention_output + jnp.einsum(
        "thd,hde->the", q_heads, prefix_b, preferred_element_type=jnp.float32
    )
    attention_output = attention_output.reshape(tok_rows, heads_dev * HEAD_WIDTH)
    square_total = lax.psum(jnp.sum(attention_output * attention_output, axis=1), "tp")
    inverse_root = lax.rsqrt(square_total / (ATTENTION_HEADS * HEAD_WIDTH) + 1e-06)[:, None]
    scaled_input = attention_output * inverse_root
    normalized_output = scaled_input * gain[None, :]
    sg = jax.nn.sigmoid(gate.astype(jnp.float32))
    gated = (normalized_output * sg).astype(jnp.bfloat16)
    cotangent = grad_out.astype(jnp.float32)
    grad_gate = (cotangent * normalized_output * sg * (1.0 - sg)).astype(jnp.bfloat16)
    normalized_gradient = cotangent * sg
    gain_gradient = lax.psum(jnp.sum(normalized_gradient * scaled_input, axis=0), "ctx")
    centered_gradient = normalized_gradient * gain[None, :]
    product_total = lax.psum(jnp.sum(centered_gradient * scaled_input, axis=1), "tp")
    product_mean = (product_total / (ATTENTION_HEADS * HEAD_WIDTH))[:, None]
    attention_gradient = (inverse_root * (centered_gradient - scaled_input * product_mean)).astype(
        jnp.bfloat16
    )
    d_heads = attention_gradient.reshape(tok_rows, heads_dev, HEAD_WIDTH)
    gstate = jnp.einsum("thd,the->hde", q_heads, d_heads, preferred_element_type=jnp.float32)
    suffix = prefix_2(gstate, "ctx", add_states, zero_state, True)
    suffix_b = suffix.astype(jnp.bfloat16)
    dscores = jnp.einsum("the,she->hts", d_heads, v_heads, preferred_element_type=jnp.float32)
    dprobs = jnp.where(causal, dscores, 0.0).astype(jnp.bfloat16)
    grad_q = jnp.einsum("hts,shd->thd", dprobs, k_heads, preferred_element_type=jnp.float32)
    grad_q = grad_q + jnp.einsum(
        "the,hde->thd", d_heads, prefix_b, preferred_element_type=jnp.float32
    )
    grad_k = jnp.einsum("hts,thd->shd", dprobs, q_heads, preferred_element_type=jnp.float32)
    grad_k = grad_k + jnp.einsum(
        "she,hde->shd", v_heads, suffix_b, preferred_element_type=jnp.float32
    )
    grad_v = jnp.einsum("hts,the->she", probs, d_heads, preferred_element_type=jnp.float32)
    grad_v = grad_v + jnp.einsum(
        "shd,hde->she", k_heads, suffix_b, preferred_element_type=jnp.float32
    )
    width = heads_dev * HEAD_WIDTH
    return (
        gated,
        grad_q.reshape(tok_rows, width).astype(jnp.bfloat16),
        grad_k.reshape(tok_rows, width).astype(jnp.bfloat16),
        grad_v.reshape(tok_rows, width).astype(jnp.bfloat16),
        grad_gate,
        gain_gradient,
    )


def solution(mesh):
    in_specs = (
        P("ctx", "tp"),
        P("ctx", "tp"),
        P("ctx", "tp"),
        P("ctx", "tp"),
        P("tp"),
        P("ctx", "tp"),
    )
    out_specs = (
        P("ctx", "tp"),
        P("ctx", "tp"),
        P("ctx", "tp"),
        P("ctx", "tp"),
        P("ctx", "tp"),
        P("tp"),
    )
    return jax.shard_map(body, mesh=mesh, in_specs=in_specs, out_specs=out_specs, check_vma=False)
```

profile of v0, /device:TPU:1, one launch (start us, length us, event | category | flops | bytes accessed | tf_op | source)
XLA Modules:
  0.0 438.1 jit_solution(3903313271888250911)
XLA Ops:
  7.2 2.6 copy.64
  9.8 2.4 copy.38
  12.3 2.5 fusion.10
  14.9 2.5 select_convert_fusion.1
  17.5 2.0 copy-done.1
  19.4 2.9 fusion.5
  22.3 136.6 %all-gather.5.cloned.1.call-done = f32[256,128,128]{2,1,0:T(8,128)} async-done(((f32[8,128,128]{2,1,0:T(8,128)}), f32[256,128,128]{2,1,0:T(8,128)}) %all-gather.5.cloned.1.call-update) | async-done | bytes 16777232 | tf_op jit(solution)/shard_map/all_gather | solution.py:12
  158.8 40.0 %while.30 = (s32[]{:T(128)}, f32[8,128,128]{2,1,0:T(8,128)S(1)}, s32[]{:T(128)}, f32[32,8,128,128]{3,2,1,0:T(8,128)}, s32[]{:T(128)}, /*index=5*/s32[]{:T(128)}) while((s32[]{:T(128)}, f32[8,128,128]{2,1,0:T(8,128)S(1)}, s32[]{:T(128)}, f32[32,8,128,128]{3,2,1,0:T(8,128)}, s32[]{:T(128)}, /*index=5*/s32[]{:T(128)}) %tuple.89), condition=%wide.region_1.2_spmd.clone, body=%wide.region_0.1_spmd.clone.sunk | while | flops 393220 | bytes 1572965 | solution.py:21
  160.1 1.2 add_select_fusion.4
  170.1 1.2 add_select_fusion.4
  183.9 1.2 add_select_fusion.4
  193.9 1.2 add_select_fusion.4
  198.9 3.5 multiply_reduce_fusion.2
  202.3 12.8 %psum.21 = f32[512]{0:T(512)S(1)} all-reduce(f32[512]{0:T(512)S(1)} %get-tuple-element.264), channel_id=1, replica_groups=mesh['ctx'=32,'tp'=8] {'tp'}, use_global_device_ids=true, to_apply=%region_3.4 | all-reduce | flops 512 | bytes 4096 | tf_op jit(solution)/shard_map/psum | solution.py:49
  215.1 3.0 copy.42
  218.1 2.9 multiply_reduce_fusion
  221.1 14.2 %psum.22 = f32[512]{0:T(512)S(1)} all-reduce(f32[512]{0:T(512)S(1)} %get-tuple-element.244), channel_id=1, replica_groups=mesh['ctx'=32,'tp'=8] {'tp'}, use_global_device_ids=true, to_apply=%region_5.6 | all-reduce | flops 512 | bytes 4096 | tf_op jit(solution)/shard_map/psum | solution.py:60
  235.3 5.0 %fusion.2 = (bf16[512,1024]{1,0:T(8,128)(2,1)}, bf16[512,1024]{1,0:T(8,128)(2,1)}, bf16[512,1024]{1,0:T(8,128)(2,1)}) fusion(bf16[512,1024]{1,0:T(8,128)(2,1)S(1)} %copy-done.8, f32[512,1024]{1,0:T(8,128)} %copy.42, f32[1024]{0:T(1024)S(1)} %copy-done.10, f32[512]{0:T(512)S(1)} %add_rsqrt_fusion, bf16[512,1024]{1,0:T(8,128)(2,1)} %param.13, ...), kind=kLoop, calls=%fused_computation.8 | loop fusion | flops 10485760 | bytes 7348224 | tf_op jit(solution)/shard_map/convert_element_type | solution.py:56
  240.3 1.5 copy.60
  243.3 2.7 select_convert_fusion
  246.0 1.5 fusion.32
  247.9 1.4 fusion.4
  249.4 2.3 copy.55
  251.7 58.5 %psum.23 = f32[1024]{0:T(1024)} all-reduce(f32[1024]{0:T(1024)S(1)} %get-tuple-element.243), channel_id=1, replica_groups=mesh['ctx'=32,'tp'=8] {'ctx'}, use_global_device_ids=true, to_apply=%region_9.10 | all-reduce | flops 1024 | bytes 8192 | tf_op jit(solution)/shard_map/psum | solution.py:58
  310.2 4.3 fusion.33
  314.4 63.8 %all-gather.7.cloned.1.call-done = f32[256,128,128]{2,1,0:T(8,128)} async-done(((f32[8,128,128]{2,1,0:T(8,128)}), f32[256,128,128]{2,1,0:T(8,128)}) %all-gather.7.cloned.1.call-update) | async-done | bytes 16777232 | tf_op jit(solution)/shard_map/all_gather | solution.py:12
  378.2 40.3 %while.31 = (s32[]{:T(128)}, f32[8,128,128]{2,1,0:T(8,128)S(1)}, s32[]{:T(128)}, f32[32,8,128,128]{3,2,1,0:T(8,128)}, s32[]{:T(128)}, /*index=5*/s32[]{:T(128)}, s32[]{:T(128)}, s32[]{:T(128)}) while((s32[]{:T(128)}, f32[8,128,128]{2,1,0:T(8,128)S(1)}, s32[]{:T(128)}, f32[32,8,128,128]{3,2,1,0:T(8,128)}, s32[]{:T(128)}, ...), condition=%wide.region_7.8_spmd.clone, body=%wide.region_6.7_spmd.clone.sunk | while | flops 393224 | bytes 1573027 | solution.py:21
  378.2 1.3 add_select_fusion.5
  379.5 1.2 add_select_fusion.5
  380.8 1.2 add_select_fusion.5
  382.1 1.2 add_select_fusion.5
  383.3 1.2 add_select_fusion.5
  384.6 1.2 add_select_fusion.5
  385.8 1.2 add_select_fusion.5
  387.1 1.2 add_select_fusion.5
  388.3 1.2 add_select_fusion.5
  389.6 1.2 add_select_fusion.5
  390.9 1.2 add_select_fusion.5
  392.1 1.2 add_select_fusion.5
  393.4 1.2 add_select_fusion.5
  394.6 1.2 add_select_fusion.5
  395.9 1.2 add_select_fusion.5
  397.1 1.2 add_select_fusion.5
  398.4 1.2 add_select_fusion.5
  399.7 1.2 add_select_fusion.5
  400.9 1.2 add_select_fusion.5
  402.2 1.2 add_select_fusion.5
  403.4 1.2 add_select_fusion.5
  404.7 1.2 add_select_fusion.5
  405.9 1.2 add_select_fusion.5
  407.2 1.2 add_select_fusion.5
  408.4 1.2 add_select_fusion.5
  409.7 1.2 add_select_fusion.5
  411.0 1.2 add_select_fusion.5
  412.2 1.2 add_select_fusion.5
  413.5 1.2 add_select_fusion.5
  414.7 1.2 add_select_fusion.5
  416.0 1.2 add_select_fusion.5
  417.2 1.2 add_select_fusion.5
  418.5 1.8 fusion.7
  421.1 1.5 add_convert_fusion
  422.6 2.4 copy.57
  425.0 4.0 fusion.3
  428.9 2.3 copy.56
  (60 shorter events, 37.3 us)
Async XLA Ops:
  7.2 7.8 %copy-start = (bf16[512,1024]{1,0:T(8,128)(2,1)S(1)}, bf16[512,1024]{1,0:T(8,128)(2,1)}, u32[]{:S(2)}) copy-start(bf16[512,1024]{1,0:T(8,128)(2,1)} %param.10) | copy-start | bytes 3145732
  7.2 151.7 %all-gather.5.cloned.1.call-start = ((), (), s32[]{:S(2)}) async-start(), calls=%async_computation | async-start | bytes 17301504 | tf_op jit(solution)/shard_map/all_gather | solution.py:12
  7.2 5.0 %copy-start.3 = (bf16[512,1024]{1,0:T(8,128)(2,1)S(1)}, bf16[512,1024]{1,0:T(8,128)(2,1)}, u32[]{:S(2)}) copy-start(bf16[512,1024]{1,0:T(8,128)(2,1)} %param.12) | copy-start | bytes 3145732
  14.8 363.4 %all-gather.7.cloned.1.call-start = ((), (), s32[]{:S(2)}) async-start(), calls=%async_computation.1 | async-start | bytes 17301504 | tf_op jit(solution)/shard_map/all_gather | solution.py:12
  17.5 2.0 copy-start.1
  215.1 3.0 copy-start.8
  215.1 3.0 copy-start.10
  243.3 2.7 copy-start.5
  246.0 1.9 copy-start.2
  378.2 40.3 %copy-start.4 = (bf16[512,1024]{1,0:T(8,128)(2,1)S(1)}, bf16[512,1024]{1,0:T(8,128)(2,1)}, u32[]{:S(2)}) copy-start(bf16[512,1024]{1,0:T(8,128)(2,1)} %param.12) | copy-start | bytes 3145732
  418.5 1.9 copy-start.6
  418.5 2.6 copy-start.9
  422.6 2.4 copy-start.7
Sparse Core Ops, SparseCore 0:
  14.9 143.9 all-gather.4
  243.4 134.7 all-gather.6
where the time goes:
time: 442 us; the launch traced here: 438 us
  waiting for transfers between devices  200 us (45%)
  other arithmetic  86.6 us (20%)
  blocking collectives  85.5 us (19%)
  matrix products  28.8 us (7%)
  local copies, waits for them, and re-layouts  20.7 us (5%)
  between operations  14.2 us (3%)
    all_gather x2, waiting for transfers between devices, prefix_2(): everything = lax.all_gather(shard, axis)  200 us
    select_n x64, other arithmetic, hop(): return jnp.where(reached, new, before)  78.6 us
    psum x1, blocking collectives, body(): lax.psum(jnp.sum(normalized_gradient * scaled_input, axis=0), 'ctx')  58.5 us
    psum x1, blocking collectives, body(): lax.psum(jnp.sum(centered_gradient * scaled_input, axis=1), 'tp')  14.2 us
    unnamed x26, local copies, waits for them, and re-layouts  12.8 us
    psum x1, blocking collectives, body(): lax.psum(jnp.sum(attention_output * attention_output, axis=1), 'tp')  12.8 us
  transfers between devices with their start and end apart: 2, of which 2 were waited for; matrix products, arithmetic and copies ran while one was open for 4% of the time, Pallas kernels for 0%

commit v1 on v0

v1 whole, which is shorter than its diff:
```python
import functools

import jax
import jax.numpy as jnp
from jax import lax
from jax.experimental import pallas as pl
from jax.experimental.pallas import tpu as pltpu
from jax.sharding import PartitionSpec as P

HEADS = 64
WIDTH = 128
MESH = pl.DeviceIdType.MESH
F32 = jnp.float32
BF16 = jnp.bfloat16
NX, NZ = 4, 8
CTX = NX * NZ
TP = 8
TOK = 512
HD = 8
FEAT_DEV = HD * WIDTH
HALVES = 2
HH = HD // HALVES
PIECE = HH * WIDTH // CTX
HALF_TOK = TOK // 2
STEPS_Z = (4, 3, -3, 2, -2, 1, -1, 0)


def dot(a, b, ca, cb):
    return lax.dot_general(a, b, (((ca,), (cb,)), ((), ())), preferred_element_type=F32)


def kernel(
    q_in, k_in, v_in, g_in, c_in, gain_ref,
    gated_out, dq_out, dk_out, dv_out, gg_out, gain_out,
    q, k, v, g, c,
    sg, w, attn, dk, dv, probs, d, pb,
    o_gated, o_dq, o_dk, o_dv, o_gg,
    l_a, r_a, p_a, s_a, l_b, r_b, p_b, s_b,
    acc_s, acc_p, rinv_c, pm_c, st, st_r, gs, gx_r, gz, gz_r,
    in_sem, out_sem,
    a_s1, a_r1, a_s2, a_r2, b_s1, b_r1, b_s2, b_r2,
    t_s, t_r, x_s, x_r, z_s, z_r,
):
    me = lax.axis_index("ctx")
    tp = lax.axis_index("tp")
    x, z = me // NZ, lax.rem(me, NZ)

    half_cols = HH * WIDTH

    def load(src, dst, sem, half):
        cols = pl.ds(half * half_cols, half_cols)
        return pltpu.make_async_copy(src.at[:, cols], dst.at[:, cols], in_sem.at[sem, half])

    pairs = ((k_in, k, 0), (v_in, v, 1), (q_in, q, 2), (g_in, g, 3), (c_in, c, 4))
    for half in range(HALVES):
        for src, dst, sem in pairs[:2]:
            load(src, dst, sem, half).start()
    for half in range(HALVES):
        for src, dst, sem in pairs[2:]:
            load(src, dst, sem, half).start()

    barrier = pltpu.get_barrier_semaphore()

    @pl.loop(1, CTX)
    def _(i):
        pl.semaphore_signal(barrier, inc=1, device_id=(lax.rem(me + i, CTX), tp), device_id_type=MESH)

    @pl.loop(1, TP)
    def _(i):
        pl.semaphore_signal(barrier, inc=1, device_id=(me, lax.rem(tp + i, TP)), device_id_type=MESH)

    def to_all(start):
        @pl.loop(0, NX)
        def _(a):
            for b, dz in enumerate(STEPS_Z):
                dx = lax.rem(2 + 3 * (a + b), NX)
                to = lax.rem(x + dx, NX) * NZ + lax.rem(z + dz + NZ, NZ)
                if dz == 0:
                    @pl.when(dx != 0)
                    def _():
                        start(to)
                else:
                    start(to)

    def remote(src, dst, ss, rs, to):
        return pltpu.make_async_remote_copy(
            src_ref=src, dst_ref=dst, send_sem=ss, recv_sem=rs, device_id=to, device_id_type=MESH
        )

    def others(buf, ss, rs):
        part = buf.at[pl.ds(0, CTX - 1)]
        return remote(part, part, ss, rs, (lax.rem(me + 1, CTX), tp))

    def send_states(half, l, r, ss, rs):
        base = half * HH * WIDTH

        def rows(j):
            return pl.ds(pl.multiple_of(base + j * PIECE, PIECE), PIECE)

        to_all(lambda j: remote(l.at[rows(j)], r.at[half, me], ss.at[half], rs.at[half], (j, tp)).start())
        r[half, me] = l[rows(me), :]

    def add_up(half, reverse, r, p, s, s1, r1, s2, r2):
        others(r.at[half], s1.at[half], r1.at[half]).wait_recv()
        total = jnp.zeros((PIECE, WIDTH), F32)
        for j in (range(CTX - 1, -1, -1) if reverse else range(CTX)):
            p[half, j] = total
            total = total + r[half, j]
        to_all(lambda j: remote(p.at[half, j], s.at[half, me], s2.at[half], r2.at[half], (j, tp)).start())
        s[half, me] = p[half, me]

    def arrived(half, s, s2, r2):
        others(s.at[half], s2.at[half], r2.at[half]).wait_recv()

    def state_of(s, half, i):
        return s[half, pl.ds(pl.multiple_of(i * (WIDTH // PIECE), WIDTH // PIECE), WIDTH // PIECE)].reshape(WIDTH, WIDTH)

    def cols_of(h):
        return pl.ds(pl.multiple_of(h * WIDTH, WIDTH), WIDTH)

    for half in range(HALVES):
        for src, dst, sem in pairs[:2]:
            load(src, dst, sem, half).wait()

        @pl.loop(half * HH, (half + 1) * HH)
        def _(h):
            cols = cols_of(h)
            l_a[cols, :] = dot(k[:, cols], v[:, cols], 0, 0)

        if half == 0:
            pl.semaphore_wait(barrier, CTX - 1 + TP - 1)
        send_states(half, l_a, r_a, a_s1, a_r1)

    lower = lax.broadcasted_iota(jnp.int32, (HALF_TOK, HALF_TOK), 0) >= lax.broadcasted_iota(
        jnp.int32, (HALF_TOK, HALF_TOK), 1
    )
    lo, hi = pl.ds(0, HALF_TOK), pl.ds(HALF_TOK, HALF_TOK)

    acc_s[...] = jnp.zeros_like(acc_s)
    acc_p[...] = jnp.zeros_like(acc_p)

    for half in range(HALVES):
        for src, dst, sem in pairs[2:]:
            load(src, dst, sem, half).wait()

        @pl.loop(half * HH, (half + 1) * HH)
        def _(h):
            cols = cols_of(h)
            q0, q1 = q[lo, cols], q[hi, cols]
            k0, k1 = k[lo, cols], k[hi, cols]
            v0, v1 = v[lo, cols], v[hi, cols]
            p00 = jnp.where(lower, dot(q0, k0, 1, 1), 0.0).astype(BF16)
            p10 = dot(q1, k0, 1, 1).astype(BF16)
            p11 = jnp.where(lower, dot(q1, k1, 1, 1), 0.0).astype(BF16)
            probs[h, 0] = p00
            probs[h, 1] = p10
            probs[h, 2] = p11
            attn[lo, cols] = dot(p00, v0, 1, 0)
            attn[hi, cols] = dot(p10, v0, 1, 0) + dot(p11, v1, 1, 0)
            gain = gain_ref[pl.ds(h, 1), :]
            for t in range(4):
                rows = pl.ds(t * 128, 128)
                gate = jax.nn.sigmoid(g[rows, cols].astype(F32))
                sg[rows, cols] = gate
                w[rows, cols] = c[rows, cols].astype(F32) * gate * gain

        add_up(half, False, r_a, p_a, s_a, a_s1, a_r1, a_s2, a_r2)

    for half in range(HALVES):
        arrived(half, s_a, a_s2, a_r2)

        @pl.loop(0, HH)
        def _(i):
            h = half * HH + i
            cols = cols_of(h)
            prefix = state_of(s_a, half, i).astype(BF16)
            pb[h] = prefix
            for t in range(4):
                rows = pl.ds(t * 128, 128)
                a = attn[rows, cols] + dot(q[rows, cols], prefix, 1, 0)
                attn[rows, cols] = a
                acc_s[rows, :] += a * a
                acc_p[rows, :] += a * w[rows, cols]

    for t in range(4):
        rows = pl.ds(t * 128, 128)
        st[pl.ds(t, 1), :] = jnp.sum(acc_s[rows, :].T, axis=0, keepdims=True)
        st[pl.ds(4 + t, 1), :] = jnp.sum(acc_p[rows, :].T, axis=0, keepdims=True)

    @pl.loop(1, TP)
    def _(i):
        remote(st, st_r.at[tp], t_s.at[0], t_r.at[0], (me, lax.rem(tp + i, TP))).start()

    st_r[tp] = st[...]
    peers = st_r.at[pl.ds(0, TP - 1)]
    peers_copy = remote(peers, peers, t_s.at[0], t_r.at[0], (me, lax.rem(tp + 1, TP)))
    peers_copy.wait_recv()
    sums = jnp.sum(st_r[...], axis=0)
    feat = float(HEADS * WIDTH)
    rinv = lax.rsqrt(sums[0:4] / feat + 1e-06)
    mean = sums[4:8] * rinv / feat
    for t in range(4):
        rows = pl.ds(t * 128, 128)
        rinv_c[rows, :] = jnp.broadcast_to(rinv[t : t + 1], (128, 128)).T
        pm_c[rows, :] = jnp.broadcast_to(mean[t : t + 1], (128, 128)).T

    for half in range(HALVES):
        @pl.loop(half * HH, (half + 1) * HH)
        def _(h):
            cols = cols_of(h)
            for t in range(4):
                rows = pl.ds(t * 128, 128)
                ri = rinv_c[rows, :]
                xhat = attn[rows, cols] * ri
                d[rows, cols] = (ri * (w[rows, cols] - xhat * pm_c[rows, :])).astype(BF16)
            l_b[cols, :] = dot(q[:, cols], d[:, cols], 0, 0)

        send_states(half, l_b, r_b, b_s1, b_r1)

    def put(src, dst, sem, half):
        cols = pl.ds(half * half_cols, half_cols)
        return pltpu.make_async_copy(src.at[:, cols], dst.at[:, cols], out_sem.at[sem, half])

    for half in range(HALVES):
        @pl.loop(half * HH, (half + 1) * HH)
        def _(h):
            cols = cols_of(h)
            gain = gain_ref[pl.ds(h, 1), :]
            part = jnp.zeros((8, WIDTH), F32)
            for t in range(4):
                rows = pl.ds(t * 128, 128)
                xhat = attn[rows, cols] * rinv_c[rows, :]
                normed = xhat * gain
                gate = sg[rows, cols]
                cot = c[rows, cols].astype(F32)
                o_gated[rows, cols] = (normed * gate).astype(BF16)
                o_gg[rows, cols] = (cot * normed * gate * (1.0 - gate)).astype(BF16)
                part = part + jnp.sum((cot * gate * xhat).reshape(16, 8, WIDTH), axis=0)
            gs[pl.ds(h, 1), :] = jnp.sum(part, axis=0, keepdims=True)

            q0, q1 = q[lo, cols], q[hi, cols]
            k0, k1 = k[lo, cols], k[hi, cols]
            v0, v1 = v[lo, cols], v[hi, cols]
            d0, d1 = d[lo, cols], d[hi, cols]
            prefix = pb[h]
            s00 = jnp.where(lower, dot(d0, v0, 1, 1), 0.0).astype(BF16)
            s10 = dot(d1, v0, 1, 1).astype(BF16)
            s11 = jnp.where(lower, dot(d1, v1, 1, 1), 0.0).astype(BF16)
            o_dq[lo, cols] = (dot(s00, k0, 1, 0) + dot(d0, prefix, 1, 1)).astype(BF16)
            o_dq[hi, cols] = (dot(s10, k0, 1, 0) + dot(s11, k1, 1, 0) + dot(d1, prefix, 1, 1)).astype(BF16)
            dk[lo, cols] = dot(s00, q0, 0, 0) + dot(s10, q1, 0, 0)
            dk[hi, cols] = dot(s11, q1, 0, 0)
            dv[lo, cols] = dot(probs[h, 0], d0, 0, 0) + dot(probs[h, 1], d1, 0, 0)
            dv[hi, cols] = dot(probs[h, 2], d1, 0, 0)

        for src, dst, sem in ((o_gated, gated_out, 0), (o_dq, dq_out, 1), (o_gg, gg_out, 4)):
            put(src, dst, sem, half).start()
        add_up(half, True, r_b, p_b, s_b, b_s1, b_r1, b_s2, b_r2)

    @pl.loop(1, NX)
    def _(i):
        to = lax.rem(x + i, NX) * NZ + z
        remote(gs, gx_r.at[x], x_s.at[0], x_r.at[0], (to, tp)).start()

    gx_r[x] = gs[...]
    xs = gx_r.at[pl.ds(0, NX - 1)]
    xs_copy = remote(xs, xs, x_s.at[0], x_r.at[0], (lax.rem(x + 1, NX) * NZ + z, tp))
    xs_copy.wait_recv()
    gz[...] = jnp.sum(gx_r[...], axis=0)

    @pl.loop(1, NZ)
    def _(i):
        to = x * NZ + lax.rem(z + i, NZ)
        remote(gz, gz_r.at[z], z_s.at[0], z_r.at[0], (to, tp)).start()

    gz_r[z] = gz[...]

    for half in range(HALVES):
        arrived(half, s_b, b_s2, b_r2)

        @pl.loop(0, HH)
        def _(i):
            cols = cols_of(half * HH + i)
            suffix = state_of(s_b, half, i).astype(BF16)
            o_dk[:, cols] = (dk[:, cols] + dot(v[:, cols], suffix, 1, 1)).astype(BF16)
            o_dv[:, cols] = (dv[:, cols] + dot(k[:, cols], suffix, 1, 0)).astype(BF16)

        put(o_dk, dk_out, 2, half).start()
        put(o_dv, dv_out, 3, half).start()

    zs = gz_r.at[pl.ds(0, NZ - 1)]
    zs_copy = remote(zs, zs, z_s.at[0], z_r.at[0], (x * NZ + lax.rem(z + 1, NZ), tp))
    zs_copy.wait_recv()
    gain_out[...] = jnp.sum(gz_r[...], axis=0)

    for half in range(HALVES):
        others(r_a.at[half], a_s1.at[half], a_r1.at[half]).wait_send()
        others(s_a.at[half], a_s2.at[half], a_r2.at[half]).wait_send()
        others(r_b.at[half], b_s1.at[half], b_r1.at[half]).wait_send()
        others(s_b.at[half], b_s2.at[half], b_r2.at[half]).wait_send()
    peers_copy.wait_send()
    xs_copy.wait_send()
    zs_copy.wait_send()
    for half in range(HALVES):
        for src, dst, sem in (
            (o_gated, gated_out, 0), (o_dq, dq_out, 1), (o_dk, dk_out, 2), (o_dv, dv_out, 3), (o_gg, gg_out, 4),
        ):
            put(src, dst, sem, half).wait()


def body(query, key_in, value, gate, gain, grad_out):
    any_space = pl.BlockSpec(memory_space=pl.ANY)
    vmem = pl.BlockSpec(memory_space=pltpu.VMEM)
    big = jax.ShapeDtypeStruct((TOK, FEAT_DEV), BF16)
    narrow = pltpu.VMEM((TOK, FEAT_DEV), BF16)
    wide = pltpu.VMEM((TOK, FEAT_DEV), F32)
    states = pltpu.VMEM((HD * WIDTH, WIDTH), F32)
    pieces = pltpu.VMEM((HALVES, CTX, PIECE, WIDTH), F32)
    column = pltpu.VMEM((TOK, WIDTH), F32)
    tile = pltpu.VMEM((8, WIDTH), F32)
    two = pltpu.SemaphoreType.DMA((HALVES,))
    one = pltpu.SemaphoreType.DMA((1,))
    scratch = (
        [narrow] * 5
        + [wide] * 5
        + [pltpu.VMEM((HD, 3, HALF_TOK, HALF_TOK), BF16), narrow, pltpu.VMEM((HD, WIDTH, WIDTH), BF16)]
        + [narrow] * 5
        + [states, pieces, pieces, pieces] * 2
        + [column] * 4
        + [tile, pltpu.VMEM((TP, 8, WIDTH), F32)]
        + [tile, pltpu.VMEM((NX, 8, WIDTH), F32), tile, pltpu.VMEM((NZ, 8, WIDTH), F32)]
        + [pltpu.SemaphoreType.DMA((5, HALVES))] * 2
        + [two] * 8
        + [one] * 6
    )
    outs = pl.pallas_call(
        kernel,
        out_shape=[big] * 5 + [jax.ShapeDtypeStruct((8, WIDTH), F32)],
        in_specs=[any_space] * 5 + [vmem],
        out_specs=[any_space] * 5 + [vmem],
        scratch_shapes=scratch,
        compiler_params=pltpu.CompilerParams(
            collective_id=0, has_side_effects=True, vmem_limit_bytes=56 * 2**20
        ),
        name="lightning",
    )(query, key_in, value, gate, grad_out, gain.reshape(8, WIDTH))
    gated, dq, dk, dv, gg, gain_gradient = outs
    return gated, dq, dk, dv, gg, gain_gradient.reshape(-1)


def solution(mesh):
    block = P("ctx", "tp")
    specs = (block, block, block, block, P("tp"), block)
    out_specs = (block, block, block, block, block, P("tp"))
    return jax.shard_map(body, mesh=mesh, in_specs=specs, out_specs=out_specs, check_vma=False)
```

time: 442 us -> 83.2 us (0.19)
  waiting for transfers between devices: 200 us -> 0 us
  other arithmetic: 86.6 us -> 0 us
  blocking collectives: 85.5 us -> 0 us
  Pallas kernels: 0 us -> 73.5 us
  matrix products: 28.8 us -> 0 us
  between operations: 14.2 us -> 0.66 us
  local copies, waits for them, and re-layouts: 20.7 us -> 8.73 us
    all_gather x2 -> x0, waiting for transfers between devices: 200 us -> none  [prefix_2(): everything = lax.all_gather(shard, axis)]
    psum x3 -> x0, blocking collectives: 85.5 us -> none  [the longest x1 58.5 us: body(): lax.psum(jnp.sum(normalized_gradient * scaled_input, axis=0), 'ctx')]
    select_n x64 -> x0, other arithmetic: 78.6 us -> none  [hop(): return jnp.where(reached, new, before)]
    pallas_call x0 -> x1, Pallas kernels: none -> 73.5 us  [body(): pl.pallas_call(kernel, out_shape=[big] * 5 + [jax.ShapeDtypeStruct((8, WI...]
    dot_general x12 -> x0, matrix products: 28.8 us -> none  [the longest x1 4.25 us: body(): jnp.einsum('hts,the->she', probs, d_heads, preferred_element_type=jnp.flo...]
    reshape x3 -> x0, local copies, waits for them, and re-layouts: 6.88 us -> none  [the longest x1 2.99 us: body(): attention_output.reshape(tok_rows, heads_dev * HEAD_WIDTH)]
    convert_element_type x1 -> x0, other arithmetic: 4.98 us -> none  [body(): (cotangent * normalized_output * sg * (1.0 - sg)).astype(jnp.bfloat16)]
    unnamed x26 -> x16, local copies, waits for them, and re-layouts: 12.8 us -> 8.73 us
  transfers between devices with their start and end apart: 2 -> 0, of which waited for: 2 -> 0; matrix products, arithmetic and copies ran while one was open for 4% -> 0% of each run, Pallas kernels for 0% -> 0%
where the time goes in v1:
time: 83.2 us; the launch traced here: 82.9 us
  Pallas kernels  73.5 us (88%)
  local copies, waits for them, and re-layouts  8.73 us (10%)
    pallas_call x1, Pallas kernels, body(): pl.pallas_call(kernel, out_shape=[big] * 5 + [jax.ShapeDtypeStruct((8, WI...  73.5 us
    unnamed x16, local copies, waits for them, and re-layouts  8.73 us

profile of v1, /device:TPU:1, one launch (start us, length us, event | category | flops | bytes accessed | tf_op | source)
XLA Modules:
  0.0 82.9 jit_solution(9880273954155633655)
XLA Ops:
  0.6 73.5 %lightning.1 = (bf16[512,1024]{1,0:T(8,128)(2,1)}, bf16[512,1024]{1,0:T(8,128)(2,1)}, bf16[512,1024]{1,0:T(8,128)(2,1)}, bf16[512,1024]{1,0:T(8,128)(2,1)}, bf16[512,1024]{1,0:T(8,128)(2,1)}, /*index=5*/f32[8,128]{1,0:T(8,128)}) custom-call(bf16[512,1024]{1,0:T(8,128)(2,1)} %q_in.1, bf16[512,1024]{1,0:T(8,128)(2,1)} %k_in.1, bf16[512,1024]{1,0:T(8,128)(2,1)} %v_in.1, ...), custom_call_target="tpu_custom_call" | custom-call | tf_op jit(solution)/shard_map/lightning/pallas_call | solution.py:336
  74.2 0.0 copy-start.3
  74.2 2.4 %copy.18 = bf16[512,1024]{1,0:T(8,128)(2,1)} copy(bf16[512,1024]{1,0:T(8,128)(2,1)} %get-tuple-element.24) | data formatting | bytes 2097152
  76.5 0.0 copy-done.3
  76.5 0.0 copy-start.2
  76.5 1.0 %copy.19 = bf16[512,1024]{1,0:T(8,128)(2,1)} copy(bf16[512,1024]{1,0:T(8,128)(2,1)S(1)} %copy-done.3) | data formatting | bytes 2097152
  77.5 0.6 copy-done.2
  78.1 0.0 copy-start.1
  78.1 1.0 %copy.20 = bf16[512,1024]{1,0:T(8,128)(2,1)} copy(bf16[512,1024]{1,0:T(8,128)(2,1)S(1)} %copy-done.2) | data formatting | bytes 2097152
  79.1 0.6 copy-done.1
  79.7 0.0 copy-start
  79.7 1.0 %copy.21 = bf16[512,1024]{1,0:T(8,128)(2,1)} copy(bf16[512,1024]{1,0:T(8,128)(2,1)S(1)} %copy-done.1) | data formatting | bytes 2097152
  80.7 0.6 copy-done
  81.3 0.0 copy-start.4
  81.3 1.0 %copy.22 = bf16[512,1024]{1,0:T(8,128)(2,1)} copy(bf16[512,1024]{1,0:T(8,128)(2,1)S(1)} %copy-done) | data formatting | bytes 2097152
  82.3 0.0 copy-done.4
  82.3 0.6 copy.23
Async XLA Ops:
  74.2 2.4 %copy-start.3 = (bf16[512,1024]{1,0:T(8,128)(2,1)S(1)}, bf16[512,1024]{1,0:T(8,128)(2,1)}, u32[]{:S(2)}) copy-start(bf16[512,1024]{1,0:T(8,128)(2,1)} %get-tuple-element.25) | copy-start | bytes 3145732
  76.5 1.6 %copy-start.2 = (bf16[512,1024]{1,0:T(8,128)(2,1)S(1)}, bf16[512,1024]{1,0:T(8,128)(2,1)}, u32[]{:S(2)}) copy-start(bf16[512,1024]{1,0:T(8,128)(2,1)} %get-tuple-element.26) | copy-start | bytes 3145732
  78.1 1.6 %copy-start.1 = (bf16[512,1024]{1,0:T(8,128)(2,1)S(1)}, bf16[512,1024]{1,0:T(8,128)(2,1)}, u32[]{:S(2)}) copy-start(bf16[512,1024]{1,0:T(8,128)(2,1)} %get-tuple-element.27) | copy-start | bytes 3145732
  79.7 1.6 %copy-start = (bf16[512,1024]{1,0:T(8,128)(2,1)S(1)}, bf16[512,1024]{1,0:T(8,128)(2,1)}, u32[]{:S(2)}) copy-start(bf16[512,1024]{1,0:T(8,128)(2,1)} %get-tuple-element.28) | copy-start | bytes 3145732
  81.3 1.0 %copy-start.4 = (f32[8,128]{1,0:T(8,128)S(1)}, f32[8,128]{1,0:T(8,128)}, u32[]{:S(2)}) copy-start(f32[8,128]{1,0:T(8,128)} %get-tuple-element.17) | copy-start | bytes 12292

commit v2 on v1

v2 whole, which is shorter than its diff:
```python
import functools

import jax
import jax.numpy as jnp
from jax import lax
from jax.experimental import pallas as pl
from jax.experimental.pallas import tpu as pltpu
from jax.sharding import PartitionSpec as P

HEADS = 64
WIDTH = 128
MESH = pl.DeviceIdType.MESH
F32 = jnp.float32
BF16 = jnp.bfloat16
NX, NZ = 4, 8
CTX = NX * NZ
TP = 8
TOK = 512
HD = 8
FEAT_DEV = HD * WIDTH
HALVES = 2
HH = HD // HALVES
GROUP = 16
PIECE = WIDTH // NX
HALF_TOK = TOK // 2


def dot(a, b, ca, cb):
    return lax.dot_general(a, b, (((ca,), (cb,)), ((), ())), preferred_element_type=F32)


def kernel(
    q_in, k_in, v_in, g_in, c_in, gain_in,
    o_gated, o_dq, o_dk, o_dv, o_gg, gain_out,
    q, k, v, g, c,
    sg, w, attn, dk, dv, probs, d, pb,
    l_a, r_a, p_a, s_a, e_a, er_a, l_b, r_b, p_b, s_b, e_b, er_b,
    acc_s, acc_p, rinv_c, pm_c, st, st_r, gs, gx_r, gz, gz_r,
    gain_ref, gain_sem, in_sem,
    t_s, t_r, x_s, x_r, z_s, z_r,
    *sems,
):
    sems_a, sems_b = sems[:6], sems[6:]
    me = lax.axis_index("ctx")
    tp = lax.axis_index("tp")
    x, z = me // NZ, lax.rem(me, NZ)

    half_cols = HH * WIDTH

    def load(src, dst, sem, half):
        cols = pl.ds(half * half_cols, half_cols)
        return pltpu.make_async_copy(src.at[:, cols], dst.at[:, cols], in_sem.at[sem, half])

    pairs = ((k_in, k, 0), (v_in, v, 1), (q_in, q, 2), (g_in, g, 3), (c_in, c, 4))
    for half in range(HALVES):
        for src, dst, sem in pairs[:2]:
            load(src, dst, sem, half).start()
    for half in range(HALVES):
        for src, dst, sem in pairs[2:]:
            load(src, dst, sem, half).start()

    gain_load = pltpu.make_async_copy(gain_in, gain_ref, gain_sem.at[0])
    gain_load.start()

    barrier = pltpu.get_barrier_semaphore()

    @pl.loop(1, CTX)
    def _(i):
        pl.semaphore_signal(barrier, inc=1, device_id=(lax.rem(me + i, CTX), tp), device_id_type=MESH)

    @pl.loop(1, TP)
    def _(i):
        pl.semaphore_signal(barrier, inc=1, device_id=(me, lax.rem(tp + i, TP)), device_id_type=MESH)

    def remote(src, dst, ss, rs, to):
        return pltpu.make_async_remote_copy(
            src_ref=src, dst_ref=dst, send_sem=ss, recv_sem=rs, device_id=to, device_id_type=MESH
        )

    class Sum:
        def __init__(self, reverse, l, r, p, s, e, e_r, s1, r1, s2, r2, s3, r3):
            self.rx = NX - 1 - x if reverse else x
            self.rz = NZ - 1 - z if reverse else z
            self.reverse = reverse
            self.l, self.r, self.p, self.s, self.e, self.e_r = l, r, p, s, e, e_r
            self.up, self.across, self.down = (s1, r1), (s2, r2), (s3, r3)
            rz = self.rz
            self.wrap = (rz == 0) | (rz == 7)
            low, mid = (rz == 1) | (rz == 2), (rz == 3) | (rz == 4)
            self.all_before, self.half_before = low | mid, self.wrap
            self.first = jnp.where(low, 0, jnp.where(mid, 2, jnp.where(self.wrap, 0, 4)))
            self.kind = jnp.where((rz == 2) | (rz == 5), 0, jnp.where((rz == 1) | (rz == 6), 1, jnp.where((rz == 4) | (rz == 7), 2, 3)))
            self.partner = jnp.where((rz == 1) | (rz == 6), 7 - rz, jnp.where((rz == 2) | (rz == 5), 7 - rz, jnp.where((rz == 0) | (rz == 3), 3 - rz, 11 - rz)))

        def device(self, rx, rz):
            ctx = rx * NZ + rz
            return (CTX - 1 - ctx if self.reverse else ctx, tp)

        def home(self, kind):
            rz = self.rz
            mid = (rz >= 2) & (rz <= 5)
            outer = jnp.where(rz < 4, 2 - kind, 5 + kind)
            inner = jnp.where(mid, 6 - kind, 21 - 7 * kind)
            place_outer = lax.rem(rz, 4)
            place_inner = jnp.where(mid, rz - 2, jnp.where(rz < 2, rz, rz - 4))
            return jnp.where(kind < 2, outer, inner), jnp.where(kind < 2, place_outer, place_inner)

        def some(self, buf, sems, half):
            part = buf.at[half, pl.ds(0, GROUP - 1)]
            return remote(part, part, sems[0].at[half], sems[1].at[half], (lax.rem(me + 1, CTX), tp))

        def send(self, half):
            base = half * HH * WIDTH

            @pl.loop(0, GROUP)
            def _(i):
                kind, hx = lax.rem(i // NX + self.rz, 4), lax.rem(lax.rem(i, NX) + self.rx, NX)
                hz, place = self.home(kind)
                rows = pl.ds(pl.multiple_of(base + kind * WIDTH + hx * PIECE, PIECE), PIECE)
                slot = self.rx * 4 + place
                mine = (hx == self.rx) & (hz == self.rz)

                @pl.when(mine)
                def _():
                    self.r[half, slot] = self.l[rows, :]

                @pl.when(jnp.logical_not(mine))
                def _():
                    remote(
                        self.l.at[rows], self.r.at[half, slot], self.up[0].at[half], self.up[1].at[half],
                        self.device(hx, hz),
                    ).start()

        def across_copy(self, half):
            return remote(
                self.e.at[half], self.e_r.at[half], self.across[0].at[half], self.across[1].at[half],
                self.device(self.rx, self.partner),
            )

        def add_up(self, half):
            self.some(self.r, self.up, half).wait_recv()
            total = jnp.zeros((PIECE, WIDTH), F32)
            for row in range(NX):
                before = total
                for m in range(4):
                    if m == 2:
                        middle = total
                    self.p[half, row * 4 + m] = total
                    total = total + self.r[half, row * 4 + m]
                self.e[half, row] = jnp.where(self.all_before, total, jnp.where(self.half_before, middle, before))
            self.across_copy(half).start()

        def finish(self, half):
            self.across_copy(half).wait_recv()
            for row in range(NX):
                whole = self.e_r[half, row]
                earlier = self.e_r[half, row - 1] if row else jnp.zeros((PIECE, WIDTH), F32)
                earlier = jnp.where(self.wrap, earlier, whole)
                for m in range(4):
                    self.p[half, row * 4 + m] += earlier if m < 2 else whole
            slot = self.kind * NX + self.rx

            @pl.loop(0, GROUP)
            def _(i):
                row, m = lax.rem(i // 4 + self.rx, NX), lax.rem(i + self.rz, 4)
                to_z = self.first + m + jnp.where(self.wrap & (m >= 2), 4, 0)
                mine = (row == self.rx) & (to_z == self.rz)

                @pl.when(mine)
                def _():
                    self.s[half, slot] = self.p[half, row * 4 + m]

                @pl.when(jnp.logical_not(mine))
                def _():
                    remote(
                        self.p.at[half, row * 4 + m], self.s.at[half, slot], self.down[0].at[half],
                        self.down[1].at[half], self.device(row, to_z),
                    ).start()

        def arrived(self, half):
            self.some(self.s, self.down, half).wait_recv()

        def state(self, half, i):
            return self.s[half, pl.ds(pl.multiple_of(i * NX, NX), NX)].reshape(WIDTH, WIDTH)

        def sent(self):
            for half in range(HALVES):
                self.some(self.r, self.up, half).wait_send()
                self.across_copy(half).wait_send()
                self.some(self.s, self.down, half).wait_send()

    prefixes = Sum(False, l_a, r_a, p_a, s_a, e_a, er_a, *sems_a)
    suffixes = Sum(True, l_b, r_b, p_b, s_b, e_b, er_b, *sems_b)

    def cols_of(h):
        return pl.ds(pl.multiple_of(h * WIDTH, WIDTH), WIDTH)

    for half in range(HALVES):
        for src, dst, sem in pairs[:2]:
            load(src, dst, sem, half).wait()

        @pl.loop(half * HH, (half + 1) * HH)
        def _(h):
            cols = cols_of(h)
            l_a[cols, :] = dot(k[:, cols], v[:, cols], 0, 0)

        if half == 0:
            pl.semaphore_wait(barrier, CTX - 1 + TP - 1)
        prefixes.send(half)

    lower = lax.broadcasted_iota(jnp.int32, (HALF_TOK, HALF_TOK), 0) >= lax.broadcasted_iota(
        jnp.int32, (HALF_TOK, HALF_TOK), 1
    )
    lo, hi = pl.ds(0, HALF_TOK), pl.ds(HALF_TOK, HALF_TOK)

    gain_load.wait()
    acc_s[...] = jnp.zeros_like(acc_s)
    acc_p[...] = jnp.zeros_like(acc_p)

    def within_forward(first, last):
        @pl.loop(first, last)
        def _(h):
            cols = cols_of(h)
            q0, q1 = q[lo, cols], q[hi, cols]
            k0, k1 = k[lo, cols], k[hi, cols]
            v0, v1 = v[lo, cols], v[hi, cols]
            p00 = jnp.where(lower, dot(q0, k0, 1, 1), 0.0).astype(BF16)
            p10 = dot(q1, k0, 1, 1).astype(BF16)
            p11 = jnp.where(lower, dot(q1, k1, 1, 1), 0.0).astype(BF16)
            probs[h, 0] = p00
            probs[h, 1] = p10
            probs[h, 2] = p11
            attn[lo, cols] = dot(p00, v0, 1, 0)
            attn[hi, cols] = dot(p10, v0, 1, 0) + dot(p11, v1, 1, 0)
            gain = gain_ref[pl.ds(h, 1), :]
            for t in range(4):
                rows = pl.ds(t * 128, 128)
                gate = jax.nn.sigmoid(g[rows, cols].astype(F32))
                sg[rows, cols] = gate
                w[rows, cols] = c[rows, cols].astype(F32) * gate * gain

    for half in range(HALVES):
        for src, dst, sem in pairs[2:]:
            load(src, dst, sem, half).wait()
    within_forward(0, 4)
    prefixes.add_up(0)
    prefixes.add_up(1)
    prefixes.finish(0)
    within_forward(4, 6)
    prefixes.finish(1)
    within_forward(6, 8)

    for half in range(HALVES):
        prefixes.arrived(half)

        @pl.loop(0, HH)
        def _(i):
            h = half * HH + i
            cols = cols_of(h)
            prefix = prefixes.state(half, i).astype(BF16)
            pb[h] = prefix
            for t in range(4):
                rows = pl.ds(t * 128, 128)
                a = attn[rows, cols] + dot(q[rows, cols], prefix, 1, 0)
                attn[rows, cols] = a
                acc_s[rows, :] += a * a
                acc_p[rows, :] += a * w[rows, cols]

    for t in range(4):
        rows = pl.ds(t * 128, 128)
        st[pl.ds(t, 1), :] = jnp.sum(acc_s[rows, :].T, axis=0, keepdims=True)
        st[pl.ds(4 + t, 1), :] = jnp.sum(acc_p[rows, :].T, axis=0, keepdims=True)

    @pl.loop(1, TP)
    def _(i):
        remote(st, st_r.at[tp], t_s.at[0], t_r.at[0], (me, lax.rem(tp + i, TP))).start()

    st_r[tp] = st[...]
    peers = st_r.at[pl.ds(0, TP - 1)]
    peers_copy = remote(peers, peers, t_s.at[0], t_r.at[0], (me, lax.rem(tp + 1, TP)))
    peers_copy.wait_recv()
    sums = jnp.sum(st_r[...], axis=0)
    feat = float(HEADS * WIDTH)
    rinv = lax.rsqrt(sums[0:4] / feat + 1e-06)
    mean = sums[4:8] * rinv / feat
    for t in range(4):
        rows = pl.ds(t * 128, 128)
        rinv_c[rows, :] = jnp.broadcast_to(rinv[t : t + 1], (128, 128)).T
        pm_c[rows, :] = jnp.broadcast_to(mean[t : t + 1], (128, 128)).T

    for half in range(HALVES):
        @pl.loop(half * HH, (half + 1) * HH)
        def _(h):
            cols = cols_of(h)
            for t in range(4):
                rows = pl.ds(t * 128, 128)
                ri = rinv_c[rows, :]
                xhat = attn[rows, cols] * ri
                d[rows, cols] = (ri * (w[rows, cols] - xhat * pm_c[rows, :])).astype(BF16)
            l_b[cols, :] = dot(q[:, cols], d[:, cols], 0, 0)

        suffixes.send(half)

    @pl.loop(0, HD)
    def _(h):
        cols = cols_of(h)
        gain = gain_ref[pl.ds(h, 1), :]
        part = jnp.zeros((8, WIDTH), F32)
        for t in range(4):
            rows = pl.ds(t * 128, 128)
            xhat = attn[rows, cols] * rinv_c[rows, :]
            normed = xhat * gain
            gate = sg[rows, cols]
            cot = c[rows, cols].astype(F32)
            o_gated[rows, cols] = (normed * gate).astype(BF16)
            o_gg[rows, cols] = (cot * normed * gate * (1.0 - gate)).astype(BF16)
            part = part + jnp.sum((cot * gate * xhat).reshape(16, 8, WIDTH), axis=0)
        gs[pl.ds(h, 1), :] = jnp.sum(part, axis=0, keepdims=True)

    @pl.loop(1, NX)
    def _(i):
        to = lax.rem(x + i, NX) * NZ + z
        remote(gs, gx_r.at[x], x_s.at[0], x_r.at[0], (to, tp)).start()

    gx_r[x] = gs[...]
    xs = gx_r.at[pl.ds(0, NX - 1)]
    xs_copy = remote(xs, xs, x_s.at[0], x_r.at[0], (lax.rem(x + 1, NX) * NZ + z, tp))

    def within_backward(first, last):
        @pl.loop(first, last)
        def _(h):
            cols = cols_of(h)
            q0, q1 = q[lo, cols], q[hi, cols]
            k0, k1 = k[lo, cols], k[hi, cols]
            v0, v1 = v[lo, cols], v[hi, cols]
            d0, d1 = d[lo, cols], d[hi, cols]
            prefix = pb[h]
            s00 = jnp.where(lower, dot(d0, v0, 1, 1), 0.0).astype(BF16)
            s10 = dot(d1, v0, 1, 1).astype(BF16)
            s11 = jnp.where(lower, dot(d1, v1, 1, 1), 0.0).astype(BF16)
            o_dq[lo, cols] = (dot(s00, k0, 1, 0) + dot(d0, prefix, 1, 1)).astype(BF16)
            o_dq[hi, cols] = (dot(s10, k0, 1, 0) + dot(s11, k1, 1, 0) + dot(d1, prefix, 1, 1)).astype(BF16)
            dk[lo, cols] = dot(s00, q0, 0, 0) + dot(s10, q1, 0, 0)
            dk[hi, cols] = dot(s11, q1, 0, 0)
            dv[lo, cols] = dot(probs[h, 0], d0, 0, 0) + dot(probs[h, 1], d1, 0, 0)
            dv[hi, cols] = dot(probs[h, 2], d1, 0, 0)

    within_backward(0, 2)
    suffixes.add_up(0)
    within_backward(2, 3)
    suffixes.add_up(1)
    xs_copy.wait_recv()
    gz[...] = jnp.sum(gx_r[...], axis=0)

    @pl.loop(1, NZ)
    def _(i):
        to = x * NZ + lax.rem(z + i, NZ)
        remote(gz, gz_r.at[z], z_s.at[0], z_r.at[0], (to, tp)).start()

    gz_r[z] = gz[...]
    suffixes.finish(0)
    within_backward(3, 5)
    suffixes.finish(1)
    within_backward(5, 8)

    for half in range(HALVES):
        suffixes.arrived(half)

        @pl.loop(0, HH)
        def _(i):
            cols = cols_of(half * HH + i)
            suffix = suffixes.state(half, i).astype(BF16)
            o_dk[:, cols] = (dk[:, cols] + dot(v[:, cols], suffix, 1, 1)).astype(BF16)
            o_dv[:, cols] = (dv[:, cols] + dot(k[:, cols], suffix, 1, 0)).astype(BF16)

    zs = gz_r.at[pl.ds(0, NZ - 1)]
    zs_copy = remote(zs, zs, z_s.at[0], z_r.at[0], (x * NZ + lax.rem(z + 1, NZ), tp))
    zs_copy.wait_recv()
    gain_out[...] = jnp.sum(gz_r[...], axis=0)

    prefixes.sent()
    suffixes.sent()
    peers_copy.wait_send()
    xs_copy.wait_send()
    zs_copy.wait_send()


def store(*refs):
    n = len(refs) // 2
    sem = refs[-1]
    srcs, dsts = refs[:n], refs[n:2 * n]

    def parts(start):
        for i, (src, dst) in enumerate(zip(srcs, dsts)):
            if src.shape[0] == TOK:
                for half in range(HALVES):
                    rows = pl.ds(half * HALF_TOK, HALF_TOK)
                    start(pltpu.make_async_copy(src.at[rows], dst.at[rows], sem.at[i, half]))
            else:
                start(pltpu.make_async_copy(src, dst, sem.at[i, 0]))

    parts(lambda copy: copy.start())
    parts(lambda copy: copy.wait())


def body(query, key_in, value, gate, gain, grad_out):
    any_space = pl.BlockSpec(memory_space=pl.ANY)
    vmem = pl.BlockSpec(memory_space=pltpu.VMEM)
    big = jax.ShapeDtypeStruct((TOK, FEAT_DEV), BF16)
    narrow = pltpu.VMEM((TOK, FEAT_DEV), BF16)
    wide = pltpu.VMEM((TOK, FEAT_DEV), F32)
    states = pltpu.VMEM((HD * WIDTH, WIDTH), F32)
    pieces = pltpu.VMEM((HALVES, GROUP, PIECE, WIDTH), F32)
    sums = pltpu.VMEM((HALVES, NX, PIECE, WIDTH), F32)
    column = pltpu.VMEM((TOK, WIDTH), F32)
    tile = pltpu.VMEM((8, WIDTH), F32)
    two = pltpu.SemaphoreType.DMA((HALVES,))
    one = pltpu.SemaphoreType.DMA((1,))
    scratch = (
        [narrow] * 5
        + [wide] * 5
        + [pltpu.VMEM((HD, 3, HALF_TOK, HALF_TOK), BF16), narrow, pltpu.VMEM((HD, WIDTH, WIDTH), BF16)]
        + [states, pieces, pieces, pieces, sums, sums] * 2
        + [column] * 4
        + [tile, pltpu.VMEM((TP, 8, WIDTH), F32)]
        + [tile, pltpu.VMEM((NX, 8, WIDTH), F32), tile, pltpu.VMEM((NZ, 8, WIDTH), F32)]
        + [tile, one, pltpu.SemaphoreType.DMA((5, HALVES))]
        + [one] * 6
        + [two] * 12
    )
    outs = pl.pallas_call(
        kernel,
        out_shape=[narrow] * 5 + [tile],
        in_specs=[any_space] * 6,
        out_specs=[vmem] * 6,
        scratch_shapes=scratch,
        compiler_params=pltpu.CompilerParams(
            collective_id=0, has_side_effects=True, vmem_limit_bytes=56 * 2**20
        ),
        name="lightning",
    )(query, key_in, value, gate, grad_out, gain.reshape(8, WIDTH))
    gated, dq, dk, dv, gg, gain_gradient = pl.pallas_call(
        store,
        out_shape=[big] * 5 + [jax.ShapeDtypeStruct((8, WIDTH), F32)],
        in_specs=[any_space] * 6,
        out_specs=[any_space] * 6,
        scratch_shapes=[pltpu.SemaphoreType.DMA((6, HALVES))],
        compiler_params=pltpu.CompilerParams(vmem_limit_bytes=4 * 2**20),
        name="store",
    )(*outs)
    return gated, dq, dk, dv, gg, gain_gradient.reshape(-1)


def solution(mesh):
    block = P("ctx", "tp")
    specs = (block, block, block, block, P("tp"), block)
    out_specs = (block, block, block, block, block, P("tp"))
    return jax.shard_map(body, mesh=mesh, in_specs=specs, out_specs=out_specs, check_vma=False)
```

time: 83.2 us -> 67.2 us (0.81)
  local copies, waits for them, and re-layouts: 8.73 us -> 0 us
  Pallas kernels: 73.5 us -> 66.4 us
    unnamed x16 -> x0, local copies, waits for them, and re-layouts: 8.73 us -> none
    pallas_call x1 -> x2, Pallas kernels: 73.5 us -> 66.4 us  [the longest x1 64 us: body(): pl.pallas_call(kernel, out_shape=[narrow] * 5 + [tile], in_specs=[any_spa...]
where the time goes in v2:
time: 67.2 us; the launch traced here: 67.1 us
  Pallas kernels  66.4 us (99%)
    pallas_call x1, Pallas kernels, body(): pl.pallas_call(kernel, out_shape=[narrow] * 5 + [tile], in_specs=[any_spa...  64 us
    pallas_call x1, Pallas kernels, body(): pl.pallas_call(store, out_shape=[big] * 5 + [jax.ShapeDtypeStruct((8, WID...  2.44 us

profile of v2, /device:TPU:1, one launch (start us, length us, event | category | flops | bytes accessed | tf_op | source)
XLA Modules:
  0.0 67.1 jit_solution(5994264887510835002)
XLA Ops:
  0.6 64.0 %lightning.1 = (bf16[512,1024]{1,0:T(8,128)(2,1)S(1)}, bf16[512,1024]{1,0:T(8,128)(2,1)S(1)}, bf16[512,1024]{1,0:T(8,128)(2,1)S(1)}, bf16[512,1024]{1,0:T(8,128)...) custom-call(bf16[512,1024]{1,0:T(8,128)(2,1)} %q_in.1, bf16[512,1024]{1,0:T(8,128)(2,1)} %k_in.1, ...), custom_call_target="tpu_custom_call" | custom-call | tf_op jit(solution)/shard_map/lightning/pallas_call | solution.py:431
  64.6 2.4 %store.1 = (bf16[512,1024]{1,0:T(8,128)(2,1)}, bf16[512,1024]{1,0:T(8,128)(2,1)}, bf16[512,1024]{1,0:T(8,128)(2,1)}, bf16[512,1024]{1,0:T(8,128)(2,1)}, bf16[512,1024]{1,0:T(8,128)(2,1)}, /*index=5*/f32[8,128]{1,0:T(8,128)}) custom-call(bf16[512,1024]{1,0:T(8,128)(2,1)S(1)} %get-tuple-element.18.refs_0_, bf16[512,1024]{1,0:T(8,128)(2,1)S(1)} %get-tuple-element.19.refs_1_, ...), custom_call_target="tpu_custom_call" | custom-call | tf_op jit(solution)/shard_map/store/pallas_call | solution.py:442

commit v3 on v2

--- a/solution.py
+++ b/solution.py
@@ -19,9 +19,11 @@
 HD = 8
 FEAT_DEV = HD * WIDTH
 HALVES = 2
-HH = HD // HALVES
+PARTS = 4
+HH = HD // PARTS
+FAR_FIRST = (2, 1, 3, 0)
 GROUP = 16
-PIECE = WIDTH // NX
+PIECE = HH * WIDTH // GROUP
 HALF_TOK = TOK // 2
 
 
@@ -45,32 +47,26 @@
     tp = lax.axis_index("tp")
     x, z = me // NZ, lax.rem(me, NZ)
 
-    half_cols = HH * WIDTH
-
-    def load(src, dst, sem, half):
-        cols = pl.ds(half * half_cols, half_cols)
-        return pltpu.make_async_copy(src.at[:, cols], dst.at[:, cols], in_sem.at[sem, half])
+    def load(src, dst, sem, part):
+        cols = pl.ds(part * HH * WIDTH, HH * WIDTH)
+        return pltpu.make_async_copy(src.at[:, cols], dst.at[:, cols], in_sem.at[sem, part])
 
     pairs = ((k_in, k, 0), (v_in, v, 1), (q_in, q, 2), (g_in, g, 3), (c_in, c, 4))
-    for half in range(HALVES):
+    for part in range(PARTS):
         for src, dst, sem in pairs[:2]:
-            load(src, dst, sem, half).start()
-    for half in range(HALVES):
+            load(src, dst, sem, part).start()
+
+    barrier = pltpu.get_barrier_semaphore()
+    for i in range(1, CTX):
+        pl.semaphore_signal(barrier, inc=1, device_id=(lax.rem(me + i, CTX), tp), device_id_type=MESH)
+    for i in range(1, TP):
+        pl.semaphore_signal(barrier, inc=1, device_id=(me, lax.rem(tp + i, TP)), device_id_type=MESH)
+
+    for part in range(PARTS):
         for src, dst, sem in pairs[2:]:
-            load(src, dst, sem, half).start()
-
+            load(src, dst, sem, part).start()
     gain_load = pltpu.make_async_copy(gain_in, gain_ref, gain_sem.at[0])
     gain_load.start()
-
-    barrier = pltpu.get_barrier_semaphore()
-
-    @pl.loop(1, CTX)
-    def _(i):
-        pl.semaphore_signal(barrier, inc=1, device_id=(lax.rem(me + i, CTX), tp), device_id_type=MESH)
-
-    @pl.loop(1, TP)
-    def _(i):
-        pl.semaphore_signal(barrier, inc=1, device_id=(me, lax.rem(tp + i, TP)), device_id_type=MESH)
 
     def remote(src, dst, ss, rs, to):
         return pltpu.make_async_remote_copy(
@@ -84,110 +80,119 @@
             self.reverse = reverse
             self.l, self.r, self.p, self.s, self.e, self.e_r = l, r, p, s, e, e_r
             self.up, self.across, self.down = (s1, r1), (s2, r2), (s3, r3)
-            rz = self.rz
-            self.wrap = (rz == 0) | (rz == 7)
-            low, mid = (rz == 1) | (rz == 2), (rz == 3) | (rz == 4)
-            self.all_before, self.half_before = low | mid, self.wrap
-            self.first = jnp.where(low, 0, jnp.where(mid, 2, jnp.where(self.wrap, 0, 4)))
-            self.kind = jnp.where((rz == 2) | (rz == 5), 0, jnp.where((rz == 1) | (rz == 6), 1, jnp.where((rz == 4) | (rz == 7), 2, 3)))
-            self.partner = jnp.where((rz == 1) | (rz == 6), 7 - rz, jnp.where((rz == 2) | (rz == 5), 7 - rz, jnp.where((rz == 0) | (rz == 3), 3 - rz, 11 - rz)))
 
         def device(self, rx, rz):
             ctx = rx * NZ + rz
             return (CTX - 1 - ctx if self.reverse else ctx, tp)
 
-        def home(self, kind):
-            rz = self.rz
-            mid = (rz >= 2) & (rz <= 5)
-            outer = jnp.where(rz < 4, 2 - kind, 5 + kind)
-            inner = jnp.where(mid, 6 - kind, 21 - 7 * kind)
-            place_outer = lax.rem(rz, 4)
-            place_inner = jnp.where(mid, rz - 2, jnp.where(rz < 2, rz, rz - 4))
-            return jnp.where(kind < 2, outer, inner), jnp.where(kind < 2, place_outer, place_inner)
-
-        def some(self, buf, sems, half):
-            part = buf.at[half, pl.ds(0, GROUP - 1)]
-            return remote(part, part, sems[0].at[half], sems[1].at[half], (lax.rem(me + 1, CTX), tp))
-
-        def send(self, half):
-            base = half * HH * WIDTH
-
-            @pl.loop(0, GROUP)
-            def _(i):
-                kind, hx = lax.rem(i // NX + self.rz, 4), lax.rem(lax.rem(i, NX) + self.rx, NX)
-                hz, place = self.home(kind)
-                rows = pl.ds(pl.multiple_of(base + kind * WIDTH + hx * PIECE, PIECE), PIECE)
-                slot = self.rx * 4 + place
-                mine = (hx == self.rx) & (hz == self.rz)
-
-                @pl.when(mine)
-                def _():
-                    self.r[half, slot] = self.l[rows, :]
-
-                @pl.when(jnp.logical_not(mine))
-                def _():
-                    remote(
-                        self.l.at[rows], self.r.at[half, slot], self.up[0].at[half], self.up[1].at[half],
-                        self.device(hx, hz),
-                    ).start()
-
-        def across_copy(self, half):
+        def some(self, buf, sems, part):
+            most = buf.at[part, pl.ds(0, GROUP - 1)]
+            return remote(most, most, sems[0].at[part], sems[1].at[part], (lax.rem(me + 1, CTX), tp))
+
+        def home(self, part, kind):
+            turn = part % 2 + 2 * (kind // 2)
+            second = lax.rem(self.rz - turn + NZ, NZ) // 4
+            start = lax.rem(turn + 4 * second, NZ)
+            off = jnp.where(second == 0, 2, 1) if kind % 2 == 0 else jnp.where(second == 0, 1, 2)
+            ahead = jnp.maximum(start - 4, 0)
+            place = jnp.where(self.rz < ahead, self.rz, self.rz - start + ahead)
+            return lax.rem(start + off, NZ), place
+
+        def role(self, part):
+            turn = part % 2
+            u = lax.rem(self.rz - turn + NZ, NZ)
+            outer_a, outer_b, inner_a = (u == 2) | (u == 5), (u == 1) | (u == 6), (u == 4) | (u == 7)
+            kind = jnp.where(outer_a, 0, jnp.where(outer_b, 1, jnp.where(inner_a, 2, 3)))
+            partner = jnp.where(kind < 2, 7 - u, jnp.where(kind == 2, 11 - u, 3 - u))
+            base = jnp.where((u == 1) | (u == 2), 0, jnp.where((u == 5) | (u == 6), 4, jnp.where((u == 3) | (u == 4), 2, 6)))
+            start = lax.rem(base + turn, NZ)
+            return kind, lax.rem(partner + turn, NZ), start, jnp.maximum(start - 4, 0)
+
+        def send(self, part):
+            first = part * HH * WIDTH
+            homes = [self.home(part, kind) for kind in range(4)]
+            for i in FAR_FIRST:
+                hx = lax.rem(self.rx + i, NX)
+                for kind, (hz, place) in enumerate(homes):
+                    rows = pl.ds(pl.multiple_of(first + (kind * NX + hx) * PIECE, PIECE), PIECE)
+                    slot = self.rx * 4 + place
+
+                    def go():
+                        remote(
+                            self.l.at[rows], self.r.at[part, slot], self.up[0].at[part], self.up[1].at[part],
+                            self.device(hx, hz),
+                        ).start()
+
+                    if i:
+                        go()
+                    else:
+                        pl.when(hz != self.rz)(go)
+
+                        @pl.when(hz == self.rz)
+                        def _():
+                            self.r[part, slot] = self.l[rows, :]
+
+        def across_copy(self, part, partner):
             return remote(
-                self.e.at[half], self.e_r.at[half], self.across[0].at[half], self.across[1].at[half],
-                self.device(self.rx, self.partner),
+                self.e.at[part], self.e_r.at[part], self.across[0].at[part], self.across[1].at[part],
+                self.device(self.rx, partner),
             )
 
-        def add_up(self, half):
-            self.some(self.r, self.up, half).wait_recv()
+        def add_up(self, part):
+            _, partner, start, ahead = self.role(part)
+            self.some(self.r, self.up, part).wait_recv()
             total = jnp.zeros((PIECE, WIDTH), F32)
+            for slot in range(GROUP):
+                self.p[part, slot] = total
+                total = total + self.r[part, slot]
+            self.p[part, GROUP] = total
+            cut = jnp.where(start < 4, 4, ahead)
             for row in range(NX):
-                before = total
+                self.e[part, row] = self.p[part, row * 4 + cut]
+            self.across_copy(part, partner).start()
+
+        def finish(self, part):
+            kind, partner, start, ahead = self.role(part)
+            self.across_copy(part, partner).wait_recv()
+            for row in range(NX):
+                whole = self.e_r[part, row]
+                earlier = self.e_r[part, row - 1] if row else jnp.zeros((PIECE, WIDTH), F32)
                 for m in range(4):
-                    if m == 2:
-                        middle = total
-                    self.p[half, row * 4 + m] = total
-                    total = total + self.r[half, row * 4 + m]
-                self.e[half, row] = jnp.where(self.all_before, total, jnp.where(self.half_before, middle, before))
-            self.across_copy(half).start()
-
-        def finish(self, half):
-            self.across_copy(half).wait_recv()
-            for row in range(NX):
-                whole = self.e_r[half, row]
-                earlier = self.e_r[half, row - 1] if row else jnp.zeros((PIECE, WIDTH), F32)
-                earlier = jnp.where(self.wrap, earlier, whole)
+                    self.p[part, row * 4 + m] += jnp.where(m < ahead, earlier, whole)
+            slot = kind * NX + self.rx
+            for i in FAR_FIRST:
+                row = lax.rem(self.rx + i, NX)
                 for m in range(4):
-                    self.p[half, row * 4 + m] += earlier if m < 2 else whole
-            slot = self.kind * NX + self.rx
-
-            @pl.loop(0, GROUP)
-            def _(i):
-                row, m = lax.rem(i // 4 + self.rx, NX), lax.rem(i + self.rz, 4)
-                to_z = self.first + m + jnp.where(self.wrap & (m >= 2), 4, 0)
-                mine = (row == self.rx) & (to_z == self.rz)
-
-                @pl.when(mine)
-                def _():
-                    self.s[half, slot] = self.p[half, row * 4 + m]
-
-                @pl.when(jnp.logical_not(mine))
-                def _():
-                    remote(
-                        self.p.at[half, row * 4 + m], self.s.at[half, slot], self.down[0].at[half],
-                        self.down[1].at[half], self.device(row, to_z),
-                    ).start()
-
-        def arrived(self, half):
-            self.some(self.s, self.down, half).wait_recv()
-
-        def state(self, half, i):
-            return self.s[half, pl.ds(pl.multiple_of(i * NX, NX), NX)].reshape(WIDTH, WIDTH)
+                    to_z = jnp.where(m < ahead, m, start + m - ahead)
+                    done = self.p.at[part, row * 4 + m]
+
+                    def go():
+                        remote(
+                            done, self.s.at[part, slot], self.down[0].at[part], self.down[1].at[part],
+                            self.device(row, to_z),
+                        ).start()
+
+                    if i:
+                        go()
+                    else:
+                        pl.when(to_z != self.rz)(go)
+
+                        @pl.when(to_z == self.rz)
+                        def _():
+                            self.s[part, slot] = self.p[part, row * 4 + m]
+
+        def arrived(self, part):
+            self.some(self.s, self.down, part).wait_recv()
+
+        def state(self, part, i):
+            whole = WIDTH // PIECE
+            return self.s[part, pl.ds(pl.multiple_of(i * whole, whole), whole)].reshape(WIDTH, WIDTH)
 
         def sent(self):
-            for half in range(HALVES):
-                self.some(self.r, self.up, half).wait_send()
-                self.across_copy(half).wait_send()
-                self.some(self.s, self.down, half).wait_send()
+            for part in range(PARTS):
+                self.some(self.r, self.up, part).wait_send()
+                self.across_copy(part, 0).wait_send()
+                self.some(self.s, self.down, part).wait_send()
 
     prefixes = Sum(False, l_a, r_a, p_a, s_a, e_a, er_a, *sems_a)
     suffixes = Sum(True, l_b, r_b, p_b, s_b, e_b, er_b, *sems_b)
@@ -195,18 +200,18 @@
     def cols_of(h):
         return pl.ds(pl.multiple_of(h * WIDTH, WIDTH), WIDTH)
 
-    for half in range(HALVES):
+    for part in range(PARTS):
         for src, dst, sem in pairs[:2]:
-            load(src, dst, sem, half).wait()
-
-        @pl.loop(half * HH, (half + 1) * HH)
+            load(src, dst, sem, part).wait()
+
+        @pl.loop(part * HH, (part + 1) * HH)
         def _(h):
             cols = cols_of(h)
             l_a[cols, :] = dot(k[:, cols], v[:, cols], 0, 0)
 
-        if half == 0:
+        if part == 0:
             pl.semaphore_wait(barrier, CTX - 1 + TP - 1)
-        prefixes.send(half)
+        prefixes.send(part)
 
     lower = lax.broadcasted_iota(jnp.int32, (HALF_TOK, HALF_TOK), 0) >= lax.broadcasted_iota(
         jnp.int32, (HALF_TOK, HALF_TOK), 1
@@ -239,25 +244,24 @@
                 sg[rows, cols] = gate
                 w[rows, cols] = c[rows, cols].astype(F32) * gate * gain
 
-    for half in range(HALVES):
+    for part in range(PARTS):
         for src, dst, sem in pairs[2:]:
-            load(src, dst, sem, half).wait()
+            load(src, dst, sem, part).wait()
     within_forward(0, 4)
-    prefixes.add_up(0)
-    prefixes.add_up(1)
-    prefixes.finish(0)
-    within_forward(4, 6)
-    prefixes.finish(1)
-    within_forward(6, 8)
-
-    for half in range(HALVES):
-        prefixes.arrived(half)
+    for part in range(PARTS):
+        prefixes.add_up(part)
+    for part in range(PARTS):
+        prefixes.finish(part)
+        within_forward(4 + part, 5 + part)
+
+    for part in range(PARTS):
+        prefixes.arrived(part)
 
         @pl.loop(0, HH)
         def _(i):
-            h = half * HH + i
+            h = part * HH + i
             cols = cols_of(h)
-            prefix = prefixes.state(half, i).astype(BF16)
+            prefix = prefixes.state(part, i).astype(BF16)
             pb[h] = prefix
             for t in range(4):
                 rows = pl.ds(t * 128, 128)
@@ -288,8 +292,8 @@
         rinv_c[rows, :] = jnp.broadcast_to(rinv[t : t + 1], (128, 128)).T
         pm_c[rows, :] = jnp.broadcast_to(mean[t : t + 1], (128, 128)).T
 
-    for half in range(HALVES):
-        @pl.loop(half * HH, (half + 1) * HH)
+    for part in range(PARTS):
+        @pl.loop(part * HH, (part + 1) * HH)
         def _(h):
             cols = cols_of(h)
             for t in range(4):
@@ -299,7 +303,7 @@
                 d[rows, cols] = (ri * (w[rows, cols] - xhat * pm_c[rows, :])).astype(BF16)
             l_b[cols, :] = dot(q[:, cols], d[:, cols], 0, 0)
 
-        suffixes.send(half)
+        suffixes.send(part)
 
     @pl.loop(0, HD)
     def _(h):
@@ -346,9 +350,8 @@
             dv[hi, cols] = dot(probs[h, 2], d1, 0, 0)
 
     within_backward(0, 2)
-    suffixes.add_up(0)
-    within_backward(2, 3)
-    suffixes.add_up(1)
+    for part in range(PARTS):
+        suffixes.add_up(part)
     xs_copy.wait_recv()
     gz[...] = jnp.sum(gx_r[...], axis=0)
 
@@ -359,17 +362,21 @@
 
     gz_r[z] = gz[...]
     suffixes.finish(0)
-    within_backward(3, 5)
+    within_backward(2, 3)
     suffixes.finish(1)
+    within_backward(3, 4)
+    suffixes.finish(2)
+    within_backward(4, 5)
+    suffixes.finish(3)
     within_backward(5, 8)
 
-    for half in range(HALVES):
-        suffixes.arrived(half)
+    for part in range(PARTS):
+        suffixes.arrived(part)
 
         @pl.loop(0, HH)
         def _(i):
-            cols = cols_of(half * HH + i)
-            suffix = suffixes.state(half, i).astype(BF16)
+            cols = cols_of(part * HH + i)
+            suffix = suffixes.state(part, i).astype(BF16)
             o_dk[:, cols] = (dk[:, cols] + dot(v[:, cols], suffix, 1, 1)).astype(BF16)
             o_dv[:, cols] = (dv[:, cols] + dot(k[:, cols], suffix, 1, 0)).astype(BF16)
 
@@ -410,23 +417,24 @@
     narrow = pltpu.VMEM((TOK, FEAT_DEV), BF16)
     wide = pltpu.VMEM((TOK, FEAT_DEV), F32)
     states = pltpu.VMEM((HD * WIDTH, WIDTH), F32)
-    pieces = pltpu.VMEM((HALVES, GROUP, PIECE, WIDTH), F32)
-    sums = pltpu.VMEM((HALVES, NX, PIECE, WIDTH), F32)
+    pieces = pltpu.VMEM((PARTS, GROUP, PIECE, WIDTH), F32)
+    totals = pltpu.VMEM((PARTS, GROUP + 1, PIECE, WIDTH), F32)
+    sums = pltpu.VMEM((PARTS, NX, PIECE, WIDTH), F32)
     column = pltpu.VMEM((TOK, WIDTH), F32)
     tile = pltpu.VMEM((8, WIDTH), F32)
-    two = pltpu.SemaphoreType.DMA((HALVES,))
+    each = pltpu.SemaphoreType.DMA((PARTS,))
     one = pltpu.SemaphoreType.DMA((1,))
     scratch = (
         [narrow] * 5
         + [wide] * 5
         + [pltpu.VMEM((HD, 3, HALF_TOK, HALF_TOK), BF16), narrow, pltpu.VMEM((HD, WIDTH, WIDTH), BF16)]
-        + [states, pieces, pieces, pieces, sums, sums] * 2
+        + [states, pieces, totals, pieces, sums, sums] * 2
         + [column] * 4
         + [tile, pltpu.VMEM((TP, 8, WIDTH), F32)]
         + [tile, pltpu.VMEM((NX, 8, WIDTH), F32), tile, pltpu.VMEM((NZ, 8, WIDTH), F32)]
-        + [tile, one, pltpu.SemaphoreType.DMA((5, HALVES))]
+        + [tile, one, pltpu.SemaphoreType.DMA((5, PARTS))]
         + [one] * 6
-        + [two] * 12
+        + [each] * 12
     )
     outs = pl.pallas_call(
         kernel,

time: 67.2 us -> 60.7 us (0.903)
  Pallas kernels: 66.4 us -> 59.9 us
    pallas_call x1, Pallas kernels: 64 us -> 57.5 us  [body(): pl.pallas_call(kernel, out_shape=[narrow] * 5 + [tile], in_specs=[any_spa...]
where the time goes in v3:
time: 60.7 us; the launch traced here: 60.6 us
  Pallas kernels  59.9 us (99%)
  between operations  0.64 us (1%)
    pallas_call x1, Pallas kernels, body(): pl.pallas_call(kernel, out_shape=[narrow] * 5 + [tile], in_specs=[any_spa...  57.5 us
    pallas_call x1, Pallas kernels, body(): pl.pallas_call(store, out_shape=[big] * 5 + [jax.ShapeDtypeStruct((8, WID...  2.44 us

profile of v3, /device:TPU:1, one launch (start us, length us, event | category | flops | bytes accessed | tf_op | source)
XLA Modules:
  0.0 60.6 jit_solution(114167188364937779)
XLA Ops:
  0.6 57.5 %lightning.1 = (bf16[512,1024]{1,0:T(8,128)(2,1)S(1)}, bf16[512,1024]{1,0:T(8,128)(2,1)S(1)}, bf16[512,1024]{1,0:T(8,128)(2,1)S(1)}, bf16[512,1024]{1,0:T(8,128)...) custom-call(bf16[512,1024]{1,0:T(8,128)(2,1)} %q_in.1, bf16[512,1024]{1,0:T(8,128)(2,1)} %k_in.1, ...), custom_call_target="tpu_custom_call" | custom-call | tf_op jit(solution)/shard_map/lightning/pallas_call | solution.py:439
  58.1 2.4 %store.1 = (bf16[512,1024]{1,0:T(8,128)(2,1)}, bf16[512,1024]{1,0:T(8,128)(2,1)}, bf16[512,1024]{1,0:T(8,128)(2,1)}, bf16[512,1024]{1,0:T(8,128)(2,1)}, bf16[512,1024]{1,0:T(8,128)(2,1)}, /*index=5*/f32[8,128]{1,0:T(8,128)}) custom-call(bf16[512,1024]{1,0:T(8,128)(2,1)S(1)} %get-tuple-element.18.refs_0_, bf16[512,1024]{1,0:T(8,128)(2,1)S(1)} %get-tuple-element.19.refs_1_, ...), custom_call_target="tpu_custom_call" | custom-call | tf_op jit(solution)/shard_map/store/pallas_call | solution.py:450

commit v4 on v3

--- a/solution.py
+++ b/solution.py
@@ -22,6 +22,8 @@
 PARTS = 4
 HH = HD // PARTS
 FAR_FIRST = (2, 1, 3, 0)
+REACH = [(dx, dz) for dx in FAR_FIRST for dz in (2, 6, 1, 7, 0) if dx or dz] + [(0, 4), (0, 3), (0, 5)]
+PEERS = [(2, 1), (2, 0), (1, 1), (3, 1), (1, 0), (3, 0), (0, 1)]
 GROUP = 16
 PIECE = HH * WIDTH // GROUP
 HALF_TOK = TOK // 2
@@ -47,6 +49,9 @@
     tp = lax.axis_index("tp")
     x, z = me // NZ, lax.rem(me, NZ)
 
+    def peer(dy, dc):
+        return lax.rem(tp // 2 + dy, TP // 2) * 2 + lax.rem(lax.rem(tp, 2) + dc, 2)
+
     def load(src, dst, sem, part):
         cols = pl.ds(part * HH * WIDTH, HH * WIDTH)
         return pltpu.make_async_copy(src.at[:, cols], dst.at[:, cols], in_sem.at[sem, part])
@@ -57,10 +62,11 @@
             load(src, dst, sem, part).start()
 
     barrier = pltpu.get_barrier_semaphore()
-    for i in range(1, CTX):
-        pl.semaphore_signal(barrier, inc=1, device_id=(lax.rem(me + i, CTX), tp), device_id_type=MESH)
-    for i in range(1, TP):
-        pl.semaphore_signal(barrier, inc=1, device_id=(me, lax.rem(tp + i, TP)), device_id_type=MESH)
+    for dx, dz in REACH:
+        to = lax.rem(x + dx, NX) * NZ + lax.rem(z + dz, NZ)
+        pl.semaphore_signal(barrier, inc=1, device_id=(to, tp), device_id_type=MESH)
+    for dy, dc in PEERS:
+        pl.semaphore_signal(barrier, inc=1, device_id=(me, peer(dy, dc)), device_id_type=MESH)
 
     for part in range(PARTS):
         for src, dst, sem in pairs[2:]:
@@ -89,11 +95,25 @@
             most = buf.at[part, pl.ds(0, GROUP - 1)]
             return remote(most, most, sems[0].at[part], sems[1].at[part], (lax.rem(me + 1, CTX), tp))
 
+        def order(self, turn):
+            u = lax.rem(self.rz - turn + NZ, NZ)
+            second, place = u // 4, lax.rem(u, 4)
+            outer = (place == 0) | (place == 3)
+            low = (place < 2) == (second == 0)
+            far = jnp.where(outer, jnp.where(low, 0, 1), jnp.where((lax.rem(u - 2 + NZ, NZ) < 4) == (lax.rem(u - 2 + NZ, 4) < 2), 2, 3))
+            inner_second, inner_place = lax.rem(u - 2 + NZ, NZ) // 4, lax.rem(u - 2 + NZ, 4)
+            stay = jnp.where(
+                outer,
+                jnp.where((inner_place == 2) == (inner_second == 0), 2, 3),
+                jnp.where((place == 2) == (second == 0), 0, 1),
+            )
+            return far, (far + 1 - 2 * lax.rem(far, 2), stay + 1 - 2 * lax.rem(stay, 2), stay)
+
         def home(self, part, kind):
             turn = part % 2 + 2 * (kind // 2)
             second = lax.rem(self.rz - turn + NZ, NZ) // 4
             start = lax.rem(turn + 4 * second, NZ)
-            off = jnp.where(second == 0, 2, 1) if kind % 2 == 0 else jnp.where(second == 0, 1, 2)
+            off = jnp.where(lax.rem(kind, 2) == second, 2, 1)
             ahead = jnp.maximum(start - 4, 0)
             place = jnp.where(self.rz < ahead, self.rz, self.rz - start + ahead)
             return lax.rem(start + off, NZ), place
@@ -110,10 +130,12 @@
 
         def send(self, part):
             first = part * HH * WIDTH
-            homes = [self.home(part, kind) for kind in range(4)]
+            turn = part % 2
+            far, near = self.order(turn)
+            homes = [(kind, *self.home(part, kind)) for kind in (far, *near)]
             for i in FAR_FIRST:
                 hx = lax.rem(self.rx + i, NX)
-                for kind, (hz, place) in enumerate(homes):
+                for kind, hz, place in homes:
                     rows = pl.ds(pl.multiple_of(first + (kind * NX + hx) * PIECE, PIECE), PIECE)
                     slot = self.rx * 4 + place
 
@@ -160,10 +182,12 @@
                 for m in range(4):
                     self.p[part, row * 4 + m] += jnp.where(m < ahead, earlier, whole)
             slot = kind * NX + self.rx
+            off = lax.rem(self.rz - start + NZ, NZ)
             for i in FAR_FIRST:
                 row = lax.rem(self.rx + i, NX)
-                for m in range(4):
-                    to_z = jnp.where(m < ahead, m, start + m - ahead)
+                for step in (3, 0, 2, 1):
+                    to_z = lax.rem(start + jnp.where(off == 1, step, 3 - step), NZ)
+                    m = jnp.where(to_z < ahead, to_z, to_z - start + ahead)
                     done = self.p.at[part, row * 4 + m]
 
                     def go():
@@ -186,7 +210,7 @@
 
         def state(self, part, i):
             whole = WIDTH // PIECE
-            return self.s[part, pl.ds(pl.multiple_of(i * whole, whole), whole)].reshape(WIDTH, WIDTH)
+            return self.s[part, i * whole : (i + 1) * whole].reshape(WIDTH, WIDTH)
 
         def sent(self):
             for part in range(PARTS):
@@ -198,19 +222,18 @@
     suffixes = Sum(True, l_b, r_b, p_b, s_b, e_b, er_b, *sems_b)
 
     def cols_of(h):
-        return pl.ds(pl.multiple_of(h * WIDTH, WIDTH), WIDTH)
+        return pl.ds(h * WIDTH if isinstance(h, int) else pl.multiple_of(h * WIDTH, WIDTH), WIDTH)
 
     for part in range(PARTS):
         for src, dst, sem in pairs[:2]:
             load(src, dst, sem, part).wait()
 
-        @pl.loop(part * HH, (part + 1) * HH)
-        def _(h):
+        for h in range(part * HH, (part + 1) * HH):
             cols = cols_of(h)
             l_a[cols, :] = dot(k[:, cols], v[:, cols], 0, 0)
 
         if part == 0:
-            pl.semaphore_wait(barrier, CTX - 1 + TP - 1)
+            pl.semaphore_wait(barrier, len(REACH) + len(PEERS))
         prefixes.send(part)
 
     lower = lax.broadcasted_iota(jnp.int32, (HALF_TOK, HALF_TOK), 0) >= lax.broadcasted_iota(
@@ -256,28 +279,27 @@
 
     for part in range(PARTS):
         prefixes.arrived(part)
-
-        @pl.loop(0, HH)
-        def _(i):
-            h = part * HH + i
-            cols = cols_of(h)
-            prefix = prefixes.state(part, i).astype(BF16)
-            pb[h] = prefix
-            for t in range(4):
-                rows = pl.ds(t * 128, 128)
-                a = attn[rows, cols] + dot(q[rows, cols], prefix, 1, 0)
+        heads = range(part * HH, (part + 1) * HH)
+        for i, h in enumerate(heads):
+            pb[h] = prefixes.state(part, i).astype(BF16)
+        for t in range(4):
+            rows = pl.ds(t * 128, 128)
+            squares, products = acc_s[rows, :], acc_p[rows, :]
+            for h in heads:
+                cols = cols_of(h)
+                a = attn[rows, cols] + dot(q[rows, cols], pb[h], 1, 0)
                 attn[rows, cols] = a
-                acc_s[rows, :] += a * a
-                acc_p[rows, :] += a * w[rows, cols]
-
-    for t in range(4):
-        rows = pl.ds(t * 128, 128)
-        st[pl.ds(t, 1), :] = jnp.sum(acc_s[rows, :].T, axis=0, keepdims=True)
-        st[pl.ds(4 + t, 1), :] = jnp.sum(acc_p[rows, :].T, axis=0, keepdims=True)
-
-    @pl.loop(1, TP)
-    def _(i):
-        remote(st, st_r.at[tp], t_s.at[0], t_r.at[0], (me, lax.rem(tp + i, TP))).start()
+                squares = squares + a * a
+                products = products + a * w[rows, cols]
+            if part < PARTS - 1:
+                acc_s[rows, :] = squares
+                acc_p[rows, :] = products
+            else:
+                st[pl.ds(t, 1), :] = jnp.sum(squares.T, axis=0, keepdims=True)
+                st[pl.ds(4 + t, 1), :] = jnp.sum(products.T, axis=0, keepdims=True)
+
+    for dy, dc in PEERS:
+        remote(st, st_r.at[tp], t_s.at[0], t_r.at[0], (me, peer(dy, dc))).start()
 
     st_r[tp] = st[...]
     peers = st_r.at[pl.ds(0, TP - 1)]
@@ -293,8 +315,7 @@
         pm_c[rows, :] = jnp.broadcast_to(mean[t : t + 1], (128, 128)).T
 
     for part in range(PARTS):
-        @pl.loop(part * HH, (part + 1) * HH)
-        def _(h):
+        for h in range(part * HH, (part + 1) * HH):
             cols = cols_of(h)
             for t in range(4):
                 rows = pl.ds(t * 128, 128)
@@ -349,9 +370,10 @@
             dv[lo, cols] = dot(probs[h, 0], d0, 0, 0) + dot(probs[h, 1], d1, 0, 0)
             dv[hi, cols] = dot(probs[h, 2], d1, 0, 0)
 
-    within_backward(0, 2)
     for part in range(PARTS):
         suffixes.add_up(part)
+        if part < PARTS - 1:
+            within_backward(part, part + 1)
     xs_copy.wait_recv()
     gz[...] = jnp.sum(gx_r[...], axis=0)
 
@@ -361,20 +383,15 @@
         remote(gz, gz_r.at[z], z_s.at[0], z_r.at[0], (to, tp)).start()
 
     gz_r[z] = gz[...]
-    suffixes.finish(0)
-    within_backward(2, 3)
-    suffixes.finish(1)
-    within_backward(3, 4)
-    suffixes.finish(2)
-    within_backward(4, 5)
-    suffixes.finish(3)
-    within_backward(5, 8)
+    for part in range(PARTS):
+        suffixes.finish(part)
+        within_backward(PARTS - 1 + part, PARTS + part)
+    within_backward(2 * PARTS - 1, HD)
 
     for part in range(PARTS):
         suffixes.arrived(part)
 
-        @pl.loop(0, HH)
-        def _(i):
+        for i in range(HH):
             cols = cols_of(part * HH + i)
             suffix = suffixes.state(part, i).astype(BF16)
             o_dk[:, cols] = (dk[:, cols] + dot(v[:, cols], suffix, 1, 1)).astype(BF16)

time: 60.7 us -> 58.3 us (0.960)
  Pallas kernels: 59.9 us -> 57.4 us
    pallas_call x1, Pallas kernels: 57.5 us -> 54.9 us  [body(): pl.pallas_call(kernel, out_shape=[narrow] * 5 + [tile], in_specs=[any_spa...]
where the time goes in v4:
time: 58.3 us; the launch traced here: 58.2 us
  Pallas kernels  57.4 us (98%)
  between operations  0.8 us (1%)
    pallas_call x1, Pallas kernels, body(): pl.pallas_call(kernel, out_shape=[narrow] * 5 + [tile], in_specs=[any_spa...  54.9 us
    pallas_call x1, Pallas kernels, body(): pl.pallas_call(store, out_shape=[big] * 5 + [jax.ShapeDtypeStruct((8, WID...  2.44 us

profile of v4, /device:TPU:1, one launch (start us, length us, event | category | flops | bytes accessed | tf_op | source)
XLA Modules:
  0.0 58.2 jit_solution(13743079067680851718)
XLA Ops:
  0.6 54.9 %lightning.1 = (bf16[512,1024]{1,0:T(8,128)(2,1)S(1)}, bf16[512,1024]{1,0:T(8,128)(2,1)S(1)}, bf16[512,1024]{1,0:T(8,128)(2,1)S(1)}, bf16[512,1024]{1,0:T(8,128)...) custom-call(bf16[512,1024]{1,0:T(8,128)(2,1)} %q_in.1, bf16[512,1024]{1,0:T(8,128)(2,1)} %k_in.1, ...), custom_call_target="tpu_custom_call" | custom-call | tf_op jit(solution)/shard_map/lightning/pallas_call | solution.py:456
  55.6 2.4 %store.1 = (bf16[512,1024]{1,0:T(8,128)(2,1)}, bf16[512,1024]{1,0:T(8,128)(2,1)}, bf16[512,1024]{1,0:T(8,128)(2,1)}, bf16[512,1024]{1,0:T(8,128)(2,1)}, bf16[512,1024]{1,0:T(8,128)(2,1)}, /*index=5*/f32[8,128]{1,0:T(8,128)}) custom-call(bf16[512,1024]{1,0:T(8,128)(2,1)S(1)} %get-tuple-element.18.refs_0_, bf16[512,1024]{1,0:T(8,128)(2,1)S(1)} %get-tuple-element.19.refs_1_, ...), custom_call_target="tpu_custom_call" | custom-call | tf_op jit(solution)/shard_map/store/pallas_call | solution.py:467

commit v5 on v4

--- a/solution.py
+++ b/solution.py
@@ -18,7 +18,6 @@
 TOK = 512
 HD = 8
 FEAT_DEV = HD * WIDTH
-HALVES = 2
 PARTS = 4
 HH = HD // PARTS
 FAR_FIRST = (2, 1, 3, 0)
@@ -57,16 +56,16 @@
         return pltpu.make_async_copy(src.at[:, cols], dst.at[:, cols], in_sem.at[sem, part])
 
     pairs = ((k_in, k, 0), (v_in, v, 1), (q_in, q, 2), (g_in, g, 3), (c_in, c, 4))
-    for part in range(PARTS):
-        for src, dst, sem in pairs[:2]:
-            load(src, dst, sem, part).start()
-
     barrier = pltpu.get_barrier_semaphore()
     for dx, dz in REACH:
         to = lax.rem(x + dx, NX) * NZ + lax.rem(z + dz, NZ)
         pl.semaphore_signal(barrier, inc=1, device_id=(to, tp), device_id_type=MESH)
     for dy, dc in PEERS:
         pl.semaphore_signal(barrier, inc=1, device_id=(me, peer(dy, dc)), device_id_type=MESH)
+
+    for part in range(PARTS):
+        for src, dst, sem in pairs[:2]:
+            load(src, dst, sem, part).start()
 
     for part in range(PARTS):
         for src, dst, sem in pairs[2:]:
@@ -416,12 +415,7 @@
 
     def parts(start):
         for i, (src, dst) in enumerate(zip(srcs, dsts)):
-            if src.shape[0] == TOK:
-                for half in range(HALVES):
-                    rows = pl.ds(half * HALF_TOK, HALF_TOK)
-                    start(pltpu.make_async_copy(src.at[rows], dst.at[rows], sem.at[i, half]))
-            else:
-                start(pltpu.make_async_copy(src, dst, sem.at[i, 0]))
+            start(pltpu.make_async_copy(src, dst, sem.at[i]))
 
     parts(lambda copy: copy.start())
     parts(lambda copy: copy.wait())
@@ -469,7 +463,7 @@
         out_shape=[big] * 5 + [jax.ShapeDtypeStruct((8, WIDTH), F32)],
         in_specs=[any_space] * 6,
         out_specs=[any_space] * 6,
-        scratch_shapes=[pltpu.SemaphoreType.DMA((6, HALVES))],
+        scratch_shapes=[pltpu.SemaphoreType.DMA((6,))],
         compiler_params=pltpu.CompilerParams(vmem_limit_bytes=4 * 2**20),
         name="store",
     )(*outs)

time: 58.3 us -> 58.2 us (level)
  no operation moved by 1% of the time
where the time goes in v5:
time: 58.2 us
  Pallas kernels  57.4 us (99%)
  between operations  0.8 us (1%)
    pallas_call x1, Pallas kernels, body(): pl.pallas_call(kernel, out_shape=[narrow] * 5 + [tile], in_specs=[any_spa...  54.9 us
    pallas_call x1, Pallas kernels, body(): pl.pallas_call(store, out_shape=[big] * 5 + [jax.ShapeDtypeStruct((8, WID...  2.41 us

profile of v5, /device:TPU:1, one launch (start us, length us, event | category | flops | bytes accessed | tf_op | source)
XLA Modules:
  0.0 58.2 jit_solution(6628101163433279733)
XLA Ops:
  0.6 54.9 %lightning.1 = (bf16[512,1024]{1,0:T(8,128)(2,1)S(1)}, bf16[512,1024]{1,0:T(8,128)(2,1)S(1)}, bf16[512,1024]{1,0:T(8,128)(2,1)S(1)}, bf16[512,1024]{1,0:T(8,128)...) custom-call(bf16[512,1024]{1,0:T(8,128)(2,1)} %q_in.1, bf16[512,1024]{1,0:T(8,128)(2,1)} %k_in.1, ...), custom_call_target="tpu_custom_call" | custom-call | tf_op jit(solution)/shard_map/lightning/pallas_call | solution.py:450
  55.6 2.4 %store.1 = (bf16[512,1024]{1,0:T(8,128)(2,1)}, bf16[512,1024]{1,0:T(8,128)(2,1)}, bf16[512,1024]{1,0:T(8,128)(2,1)}, bf16[512,1024]{1,0:T(8,128)(2,1)}, bf16[512,1024]{1,0:T(8,128)(2,1)}, /*index=5*/f32[8,128]{1,0:T(8,128)}) custom-call(bf16[512,1024]{1,0:T(8,128)(2,1)S(1)} %get-tuple-element.18.refs_0_, bf16[512,1024]{1,0:T(8,128)(2,1)S(1)} %get-tuple-element.19.refs_1_, ...), custom_call_target="tpu_custom_call" | custom-call | tf_op jit(solution)/shard_map/store/pallas_call | solution.py:461

commit v6 on v5

--- a/solution.py
+++ b/solution.py
@@ -175,19 +175,17 @@
         def finish(self, part):
             kind, partner, start, ahead = self.role(part)
             self.across_copy(part, partner).wait_recv()
-            for row in range(NX):
-                whole = self.e_r[part, row]
-                earlier = self.e_r[part, row - 1] if row else jnp.zeros((PIECE, WIDTH), F32)
-                for m in range(4):
-                    self.p[part, row * 4 + m] += jnp.where(m < ahead, earlier, whole)
             slot = kind * NX + self.rx
             off = lax.rem(self.rz - start + NZ, NZ)
             for i in FAR_FIRST:
                 row = lax.rem(self.rx + i, NX)
+                whole = self.e_r[part, row]
+                earlier = jnp.where(row > 0, self.e_r[part, jnp.maximum(row - 1, 0)], 0.0)
                 for step in (3, 0, 2, 1):
                     to_z = lax.rem(start + jnp.where(off == 1, step, 3 - step), NZ)
                     m = jnp.where(to_z < ahead, to_z, to_z - start + ahead)
                     done = self.p.at[part, row * 4 + m]
+                    done[...] += jnp.where(m < ahead, earlier, whole)
 
                     def go():
                         remote(

time: 58.2 us -> 58.3 us (level)
  no operation moved by 1% of the time
where the time goes in v6:
time: 58.3 us; the launch traced here: 58.2 us
  Pallas kernels  57.4 us (98%)
  between operations  0.8 us (1%)
    pallas_call x1, Pallas kernels, body(): pl.pallas_call(kernel, out_shape=[narrow] * 5 + [tile], in_specs=[any_spa...  55 us
    pallas_call x1, Pallas kernels, body(): pl.pallas_call(store, out_shape=[big] * 5 + [jax.ShapeDtypeStruct((8, WID...  2.41 us

profile of v6, /device:TPU:1, one launch (start us, length us, event | category | flops | bytes accessed | tf_op | source)
XLA Modules:
  0.0 58.2 jit_solution(9891729173055173915)
XLA Ops:
  0.6 55.0 %lightning.1 = (bf16[512,1024]{1,0:T(8,128)(2,1)S(1)}, bf16[512,1024]{1,0:T(8,128)(2,1)S(1)}, bf16[512,1024]{1,0:T(8,128)(2,1)S(1)}, bf16[512,1024]{1,0:T(8,128)...) custom-call(bf16[512,1024]{1,0:T(8,128)(2,1)} %q_in.1, bf16[512,1024]{1,0:T(8,128)(2,1)} %k_in.1, ...), custom_call_target="tpu_custom_call" | custom-call | tf_op jit(solution)/shard_map/lightning/pallas_call | solution.py:448
  55.6 2.4 %store.1 = (bf16[512,1024]{1,0:T(8,128)(2,1)}, bf16[512,1024]{1,0:T(8,128)(2,1)}, bf16[512,1024]{1,0:T(8,128)(2,1)}, bf16[512,1024]{1,0:T(8,128)(2,1)}, bf16[512,1024]{1,0:T(8,128)(2,1)}, /*index=5*/f32[8,128]{1,0:T(8,128)}) custom-call(bf16[512,1024]{1,0:T(8,128)(2,1)S(1)} %get-tuple-element.18.refs_0_, bf16[512,1024]{1,0:T(8,128)(2,1)S(1)} %get-tuple-element.19.refs_1_, ...), custom_call_target="tpu_custom_call" | custom-call | tf_op jit(solution)/shard_map/store/pallas_call | solution.py:459
